TPU v7x, 512 devices: a whole 4x4x16 slice. The times are simulated.
512 devices in a mesh: dp: 128 (over x, z, core), rep: 4 (over y).
Axes of the slice: x: 4, y: 4, z: 16, core: 2. Of those that a mesh axis runs over, the one named last changes fastest.
Arguments:
- ratings: bfloat16 [1024, 12800], P(('dp', 'rep')), may hold values from -6 to 6
- confidence: bfloat16 [1024, 12800], P(('dp', 'rep')), may hold values from 1 to 20
- rated: int32 [1024, 200], P(('dp', 'rep')), may hold values 0 or 1
- item_factors: bfloat16 [1048576, 128], P(('dp', 'rep')), may hold values from -0.0546875 to 0.0546875
- cold_owner: int32 [128, 4, 192, 1], P('dp', 'rep'), may hold values from 0 to 127; in each aligned block of 192 rows (0 to 191, 192 to 383, ..., all dimensions but the last counted through in order) at most 2 rows name the same one
- cold_local: int32 [128, 4, 192], P('dp', 'rep'), may hold values from 0 to 127
- hot_group: int32 [8], replicated, may hold values from 0 to 127, as said below
- hot_local: int32 [8], replicated, may hold values from 0 to 127
Outputs:
- user_factors: float32 [1024, 128], P(('dp', 'rep'))
Inputs may be any that keep to these rules, and one draw needn't show every extreme that they name: `cold_owner`: on each device, no owner group is named by more than 2 of its 192 rows; some group is named exactly 2 times. `hot_group`: the hot blocks' owner groups are distinct.
All inputs are finite; a program needn't handle non-finite values. No bound on the sum of `rated` on one device may be relied on, other than what follows from the above.
Results may differ from a plain program's by a relative error of at most 0.0029.
Values may be sent and summed in bfloat16 or wider, within the bound.
A program may use at most 64 MiB of HBM per device.

v0:
```python
import jax
import jax.numpy as jnp
from jax import lax
from jax.sharding import PartitionSpec as P

BLK = 64
CAP = 2
ITERS = 3


def broadcast(value, axis, source):
    kept = jnp.where(lax.axis_index(axis) == source, value, 0).astype(value.dtype)
    return lax.psum(kept, axis)


def conjugate(gram_stack, right_side):
    highest = lax.Precision.HIGHEST
    solution = jnp.zeros_like(right_side)
    residual = right_side
    direction = right_side
    norm_now = jnp.sum(residual * residual, axis=-1)
    for iteration in range(ITERS):
        images = jnp.einsum("urs,us->ur", gram_stack, direction, precision=highest)
        step_size = norm_now / jnp.sum(direction * images, axis=-1)
        solution = solution + step_size[:, None] * direction
        residual = residual - step_size[:, None] * images
        norm_next = jnp.sum(residual * residual, axis=-1)
        direction = residual + (norm_next / norm_now)[:, None] * direction
        norm_now = norm_next
    return solution


def body(ratings, confidence, rated, item_factors, cold_owner, cold_local, hot_group, hot_local):
    dp_count = lax.axis_size("dp")
    factor_width = item_factors.shape[1]
    block_rows = BLK
    group_rows = lax.all_gather(item_factors, "rep", axis=0, tiled=True)
    group_table = group_rows.reshape(-1, block_rows * factor_width)
    group_blocks = group_table.shape[0]
    owners = cold_owner.reshape(-1)
    local_ids = cold_local.reshape(-1)
    matches = (owners[:, None] == jnp.arange(dp_count, dtype=jnp.int32)[None, :]).astype(jnp.int32)
    before = jnp.cumsum(matches, axis=0) - matches
    slot_of = jnp.sum(before * matches, axis=1)
    slot_count = CAP
    position = owners * slot_count + slot_of
    wanted = jnp.full((dp_count * slot_count,), -1, jnp.int32).at[position].set(local_ids)
    requested = lax.all_to_all(
        wanted.reshape(dp_count, slot_count), "dp", split_axis=0, concat_axis=0, tiled=True
    )
    flat_ids = jnp.clip(requested.reshape(-1), 0, group_blocks - 1)
    served = jnp.take(group_table, flat_ids, axis=0).reshape(
        dp_count, slot_count, block_rows, factor_width
    )
    arrived = lax.all_to_all(served, "dp", split_axis=0, concat_axis=0, tiled=True).reshape(
        dp_count * slot_count, block_rows * factor_width
    )
    cold_items = jnp.take(arrived, position, axis=0)
    pieces = []
    for index_hot in range(hot_group.shape[0]):
        own_block = jnp.take(group_table, hot_local[index_hot], axis=0)
        pieces.append(broadcast(own_block, "dp", hot_group[index_hot]))
    hot_items = jnp.stack(pieces)
    item_rows = jnp.concatenate([cold_items, hot_items], axis=0).reshape(-1, factor_width)
    user_count = confidence.shape[0]
    weights = (
        confidence.astype(jnp.float32).reshape(user_count, -1, block_rows)
        * rated.astype(jnp.float32)[:, :, None]
    ).reshape(user_count, -1)

    def one_user(user_pair):
        weight_row, rating_row = user_pair
        scaled = (weight_row[:, None] * item_rows.astype(jnp.float32)).astype(jnp.bfloat16)
        gram_matrix = lax.dot_general(
            scaled, item_rows, (((0,), (0,)), ((), ())), preferred_element_type=jnp.float32
        )
        right_side = jnp.dot(rating_row, scaled, preferred_element_type=jnp.float32)
        return (gram_matrix, right_side)

    gram_stack, right_side = lax.map(one_user, (weights, ratings))
    gram_stack = gram_stack + 0.1 * jnp.eye(factor_width, dtype=jnp.float32)[None, :, :]
    return conjugate(gram_stack, right_side)


def solution(mesh):
    in_specs = (
        P(("dp", "rep"), None),
        P(("dp", "rep"), None),
        P(("dp", "rep"), None),
        P(("dp", "rep"), None),
        P("dp", "rep", None, None),
        P("dp", "rep", None),
        P(),
        P(),
    )
    out_specs = P(("dp", "rep"), None)
    return jax.shard_map(body, mesh=mesh, in_specs=in_specs, out_specs=out_specs, check_vma=False)
```

profile of v0, /device:TPU:6, one launch (start us, length us, event | category | flops | bytes accessed | tf_op | source)
XLA Modules:
  0.0 532.1 jit_solution(11848023008502417033)
XLA Ops:
  9.8 1.3 scatter_custom_fusion
  11.3 33.0 %all_to_all.14 = s32[128,1,2]{2,1,0:T(1,128)S(1)} all-to-all(s32[128,1,2]{2,1,0:T(1,128)S(1)} %bitcast.85), channel_id=1, replica_groups=mesh['dp'=128,'rep'=4] {'dp'}, dimensions={0} | all-to-all | bytes 2048 | tf_op jit(solution)/shard_map/all_to_all | solution.py:48
  44.8 7.6 %all-gather.2.cloned.1.call-done = bf16[8192,128]{1,0:T(8,128)(2,1)} async-done(((bf16[2048,128]{1,0:T(8,128)(2,1)}), bf16[8192,128]{1,0:T(8,128)(2,1)}) %all-gather.2.cloned.1.call-update) | async-done | bytes 2097168 | tf_op jit(solution)/shard_map/all_gather | solution.py:37
  52.4 2.8 reshape.152
  55.3 5.1 gather_fusion
  60.4 3.4 copy.20
  63.8 2.3 broadcast_select_fusion
  66.1 17.6 %all-to-all-start.1 = ((bf16[128,2,64,128]{3,2,1,0:T(8,128)(2,1)}), bf16[128,2,64,128]{3,2,1,0:T(8,128)(2,1)}, u32[]{:S(2)}, u32[]{:S(2)}) async-start(bf16[128,2,64,128]{3,2,1,0:T(8,128)(2,1)} %broadcast_select_fusion), calls=%async_computation.1 | async-start | bytes 8388608 | tf_op jit(solution)/shard_map/all_to_all | solution.py:55
  105.5 0.9 fusion.30
  111.4 159.5 %all-to-all-done.1 = bf16[128,2,64,128]{3,2,1,0:T(8,128)(2,1)} async-done(((bf16[128,2,64,128]{3,2,1,0:T(8,128)(2,1)}), bf16[128,2,64,128]{3,2,1,0:T(8,128)(2,1)}, u32[]{:S(2)}, u32[]{:S(2)}) %all-to-all-start.1) | async-done | bytes 4194336 | tf_op jit(solution)/shard_map/all_to_all | solution.py:55
  270.8 12.3 %copy.25 = bf16[32,8,64,128]{3,1,2,0:T(8,128)(2,1)} copy(bf16[32,8,64,128]{3,2,1,0:T(8,128)(2,1)} %bitcast.51) | data formatting | bytes 8388608
  283.1 8.3 %gather_fusion.1 = bf16[192,8192]{1,0:T(8,128)(2,1)S(1)} fusion(bf16[256,8192]{1,0:T(8,128)(2,1)} %bitcast.77, s32[1024]{0:T(1024)S(1)} %pad_clamp_fusion), kind=kCustom, calls=%fused_computation.1 | custom fusion | bytes 6292224 | tf_op jit(solution)/shard_map/jit(_take)/gather | solution.py:58
  291.5 2.0 broadcast_select_fusion.1
  293.5 189.2 %all-reduce.4.cloned.1.call-done = (bf16[1,8192]{1,0:T(2,128)(2,1)}, bf16[1,8192]{1,0:T(2,128)(2,1)}, bf16[1,8192]{1,0:T(2,128)(2,1)}, bf16[1,8192]{1,0:T(2,128)...) async-done(((bf16[1,8192]{1,0:T(2,128)(2,1)}, bf16[1,8192]{1,0:T(2,128)(2,1)}, ...) | async-done | bytes 131088 | tf_op jit(solution)/shard_map/psum | solution.py:13
  482.7 12.5 %concatenate.3 = bf16[200,8192]{1,0:T(8,128)(2,1)S(1)} concatenate(bf16[192,8192]{1,0:T(8,128)(2,1)} %broadcast_select_fusion.1, bf16[1,8192]{1,0:T(2,128)(2,1)} %get-tuple-element.74, bf16[1,8192]{1,0:T(2,128)(2,1)} %get-tuple-element.75, bf16[1,8192]{1,0:T(2,128)(2,1)} %get-tuple-element.76, bf16[1,8192]{1,0:T(2,128)(2,1)} %get-tuple-element.77, ...), dimensions={0} | concatenate | bytes 6553600 | tf_op jit(solution)/shard_map/concatenate | solution.py:64
  495.2 3.5 reshape.154
  498.6 21.3 %while.13 = (s32[]{:T(128)}, f32[2,128,128]{2,1,0:T(8,128)}, f32[2,128]{1,0:T(2,128)S(1)}, f32[2,12800]{1,0:T(2,128)S(1)}, bf16[12800,128]{1,0:T(8,128)(2,1)}, /...) while((s32[]{:T(128)}, f32[2,128,128]{2,1,0:T(8,128)}, f32[2,128]{1,0:T(2,128)S(1)}, ...), condition=%wide.region_13.15_spmd, body=%wide.region_12.14_spmd.sunk | while | flops 432537600 | bytes 23263356 | solution.py:80
  498.8 7.0 %fusion.47 = f32[1,128]{1,0:T(1,128)S(1)} fusion(bf16[12800,128]{1,0:T(8,128)(2,1)} %get-tuple-element.169, f32[12800]{0:T(1024)S(1)} %dynamic-slice_reduce_fusion.2, bf16[2,12800]{1,0:T(2,128)(2,1)} %get-tuple-element.170, s32[]{:T(128)} %get-tuple-element.157), kind=kOutput, calls=%fused_computation.4.clone.1 | convolution fusion | flops 8192000 | bytes 3379716 | tf_op jit(solution)/shard_map/while/body/eval_jaxpr/dot_general | solution.py:77
  505.8 3.5 fusion.46
  509.4 7.0 %fusion.47 = f32[1,128]{1,0:T(1,128)S(1)} fusion(bf16[12800,128]{1,0:T(8,128)(2,1)} %get-tuple-element.169, f32[12800]{0:T(1024)S(1)} %dynamic-slice_reduce_fusion.2, bf16[2,12800]{1,0:T(2,128)(2,1)} %get-tuple-element.170, s32[]{:T(128)} %get-tuple-element.157), kind=kOutput, calls=%fused_computation.4.clone.1 | convolution fusion | flops 8192000 | bytes 3379716 | tf_op jit(solution)/shard_map/while/body/eval_jaxpr/dot_general | solution.py:77
  516.5 3.4 fusion.46
  519.9 1.2 fusion.15
  521.6 1.2 fusion.13
  523.2 1.2 fusion.11
  (75 shorter events, 12.7 us)
Async XLA Ops:
  6.5 45.9 %all-gather.2.cloned.1.call-start = ((), (), s32[]{:S(2)}) async-start(), calls=%async_computation.2 | async-start | bytes 2621440 | tf_op jit(solution)/shard_map/all_gather | solution.py:37
  66.0 17.9 %copy-start.2 = (s32[8]{0:T(128)S(1)}, s32[8]{0:T(128)}, u32[]{:S(2)}) copy-start(s32[8]{0:T(128)} %param.19) | copy-start | bytes 100
  66.0 33.3 %copy-start.3 = (s32[8]{0:T(128)S(1)}, s32[8]{0:T(128)}, u32[]{:S(2)}) copy-start(s32[8]{0:T(128)} %param.18) | copy-start | bytes 100
  66.0 39.0 %copy-start.5 = (s32[2,200]{1,0:T(2,128)S(1)}, s32[2,200]{1,0:T(2,128)}, u32[]{:S(2)}) copy-start(s32[2,200]{1,0:T(2,128)} %param.14) | copy-start | bytes 4804
  66.0 39.4 %copy-start.4 = (s32[1,1,192,1]{2,3,1,0:T(1,128)S(1)}, s32[1,1,192,1]{2,3,1,0:T(1,128)}, u32[]{:S(2)}) copy-start(s32[1,1,192,1]{2,3,1,0:T(1,128)} %param.16) | copy-start | bytes 2308
  66.0 39.4 %copy-start.1 = (bf16[2,12800]{1,0:T(2,128)(2,1)S(1)}, bf16[2,12800]{1,0:T(2,128)(2,1)}, u32[]{:S(2)}) copy-start(bf16[2,12800]{1,0:T(2,128)(2,1)} %param.13) | copy-start | bytes 153604
  66.1 204.8 %all-to-all-start.1 = ((bf16[128,2,64,128]{3,2,1,0:T(8,128)(2,1)}), bf16[128,2,64,128]{3,2,1,0:T(8,128)(2,1)}, u32[]{:S(2)}, u32[]{:S(2)}) async-start(bf16[128,2,64,128]{3,2,1,0:T(8,128)(2,1)} %broadcast_select_fusion), calls=%async_computation.1 | async-start | bytes 8388608 | tf_op jit(solution)/shard_map/all_to_all | solution.py:55
  83.7 399.0 %all-reduce.4.cloned.1.call-start = ((), (), s32[]{:S(2)}) async-start(), calls=%async_computation.3 | async-start | bytes 524288 | tf_op jit(solution)/shard_map/psum | solution.py:13
  498.6 7.2 %copy-start = (bf16[12800,128]{1,0:T(8,128)(2,1)S(1)}, bf16[12800,128]{1,0:T(8,128)(2,1)}, u32[]{:S(2)}) copy-start(bf16[12800,128]{1,0:T(8,128)(2,1)} %get-tuple-element.169) | copy-start | bytes 9830404 | tf_op jit(solution)/shard_map/while
  509.3 7.2 %copy-start = (bf16[12800,128]{1,0:T(8,128)(2,1)S(1)}, bf16[12800,128]{1,0:T(8,128)(2,1)}, u32[]{:S(2)}) copy-start(bf16[12800,128]{1,0:T(8,128)(2,1)} %get-tuple-element.169) | copy-start | bytes 9830404 | tf_op jit(solution)/shard_map/while
Sparse Core Ops, SparseCore 0:
  9.5 42.9 all-gather.1
  111.5 371.1 all-reduce.3
where the time goes:
time: 534 us; the launch traced here: 532 us
  waiting for transfers between devices  357 us (67%)
  local copies, waits for them, and re-layouts  56.4 us (11%)
  between operations  33.5 us (6%)
  blocking collectives  33 us (6%)
  matrix products  24.6 us (5%)
  starting transfers between devices  17.8 us (3%)
  other arithmetic  9.7 us (2%)
    psum x1, waiting for transfers between devices, broadcast(): return lax.psum(kept, axis)  189 us
    all_to_all x1, waiting for transfers between devices, body(): lax.all_to_all(served, 'dp', split_axis=0, concat_axis=0, tiled=True)  159 us
    all_to_all x1, blocking collectives, body(): lax.all_to_all(wanted.reshape(dp_count, slot_count), 'dp', split_axis=0,...  33 us
    all_to_all x1, starting transfers between devices, body(): lax.all_to_all(served, 'dp', split_axis=0, concat_axis=0, tiled=True)  17.6 us
    unnamed x13, local copies, waits for them, and re-layouts  15.7 us
    dot_general x2, matrix products, one_user(): right_side = jnp.dot(rating_row, scaled, preferred_element_type=jnp.float32)  14 us
    concatenate x1, local copies, waits for them, and re-layouts, body(): jnp.concatenate([cold_items, hot_items], axis=0).reshape(-1, factor_width)  12.5 us
  transfers between devices with their start and end apart: 3, of which 3 were waited for; matrix products, arithmetic and copies ran while one was open for 6% of the time, Pallas kernels for 0%

commit v1 on v0

v1 whole, which is shorter than its diff:
```python
import functools

import jax
import jax.numpy as jnp
from jax import lax
from jax.experimental import pallas as pl
from jax.experimental.pallas import tpu as pltpu
from jax.sharding import PartitionSpec as P

BLK = 64
CAP = 2
ITERS = 3
N_X = 4
MESH = pl.DeviceIdType.MESH
bf16, f32, i32 = jnp.bfloat16, jnp.float32, jnp.int32


def prepare(n_x, n_z, ratings, confidence, rated, cold_owner, cold_local, hot_group):
    pairs = n_x * n_z
    owners = cold_owner.reshape(-1)
    local_ids = cold_local.reshape(-1)
    cold = owners.shape[0]
    order = jnp.arange(cold, dtype=i32)
    same = (owners[:, None] == owners[None, :]) & (order[None, :] < order[:, None])
    slot_of = jnp.sum(same.astype(i32), axis=1)
    position = owners * CAP + slot_of
    match = position[None, :] == jnp.arange(2 * pairs * CAP, dtype=i32)[:, None]
    users = confidence.shape[0]
    weights = confidence.reshape(users, -1, BLK) * rated.astype(bf16)[:, :, None]
    both = jnp.concatenate([weights, ratings.reshape(users, -1, BLK)], axis=0)
    both = both.transpose(1, 0, 2).reshape(-1, 2 * users * BLK)
    cold_part = jnp.dot(match.astype(bf16), both[:cold], preferred_element_type=f32).astype(bf16)
    cold_part = cold_part.reshape(n_x, n_z, 2 * CAP, 2 * users, BLK).transpose(1, 0, 3, 2, 4)
    cold_part = cold_part.reshape(n_z, n_x, 2 * users, CAP, 2 * BLK)
    hot_match = hot_group[None, :] == jnp.arange(2 * pairs, dtype=i32)[:, None]
    hot_part = jnp.dot(hot_match.astype(bf16), both[cold:], preferred_element_type=f32).astype(bf16)
    hot_part = hot_part.reshape(n_x, n_z, 2, 2 * users, BLK).transpose(1, 0, 3, 2, 4)
    hot_part = hot_part.reshape(n_z, n_x, 2 * users, 1, 2 * BLK)
    message = jnp.concatenate([cold_part, hot_part], axis=3).reshape(n_z, n_x, 6 * users, 2 * BLK)
    message = jnp.pad(message, ((0, 0), (0, 0), (0, 16 - 6 * users), (0, 0)))
    ids = jnp.sum(jnp.where(match, local_ids[None, :], 0), axis=1)
    ids = ids.reshape(n_x, n_z, 1, 2 * CAP).transpose(1, 0, 2, 3)
    ids = jnp.pad(ids, ((0, 0), (0, 0), (0, 0), (0, 128 - 2 * CAP)))
    return message, ids


def kernel(n_x, n_z, message, ids, items, hot_id, out,
           table, msg_z, msg_x, ids_z, ids_x, ids_s, gram, part, mid, red_x, red_z, dir_z, dir_x,
           y_send, y_recv, c_send, c_recv, l_sem,
           a_send, a_recv, b_send, b_recv, zs_sem, zr_sem, xs_sem, xr_sem):
    dp = lax.axis_index("dp")
    y = lax.axis_index("rep")
    core = dp % 2
    z = (dp // 2) % n_z
    x = dp // (2 * n_z)
    n_y = 4

    def at(x_to, z_to):
        return ((x_to * n_z + z_to) * 2 + core, y)

    up, down, far = (y + 1) % n_y, (y + n_y - 1) % n_y, (y + 2) % n_y
    up_id, down_id, mate_id = (dp, up), (dp, down), (x * n_z * 2 + z * 2 + 1 - core, y)

    def remote(src, dst, send, recv, to):
        return pltpu.make_async_remote_copy(
            src_ref=src, dst_ref=dst, send_sem=send, recv_sem=recv, device_id=to, device_id_type=MESH)

    def each(count, body):
        for k in range(1, count):
            body(k)

    def others(ref, lead=()):
        index = lead + (pl.ds(0, ref.shape[len(lead)] - 1),)
        return ref.at[index]

    def waiter(ref, send, recv):
        return remote(ref, ref, send, recv, mate_id)

    barrier = pltpu.get_barrier_semaphore()
    for to in (up_id, down_id, mate_id):
        pl.semaphore_signal(barrier, inc=1, device_id=to, device_id_type=MESH)
    each(n_z, lambda k: pl.semaphore_signal(
        barrier, inc=1, device_id=at(x, (z + k) % n_z), device_id_type=MESH))
    each(n_x, lambda k: pl.semaphore_signal(
        barrier, inc=1, device_id=at((x + k) % n_x, z), device_id_type=MESH))
    pl.semaphore_wait(barrier, 3 + n_z - 1 + n_x - 1)

    held = items.shape[0]
    half = held // 2

    def rows(of_core, of_y, h):
        return table.at[of_core, pl.ds(of_y * held + h * half, half)]

    def own(h):
        return items.at[pl.ds(h * half, half)]

    def up_copy(k):
        if k < 2:
            return remote(own(k), rows(core, y, k), y_send.at[k], y_recv.at[k], up_id)
        return remote(rows(core, down, 0), rows(core, down, 0), y_send.at[2], y_recv.at[2], up_id)

    def down_copy(k):
        if k < 2:
            return remote(own(1 - k), rows(core, y, 1 - k), y_send.at[3 + k], y_recv.at[3 + k], down_id)
        return remote(rows(core, up, 1), rows(core, up, 1), y_send.at[5], y_recv.at[5], down_id)

    def from_down(k):
        ref = rows(core, down, k) if k < 2 else rows(core, far, 0)
        return remote(ref, ref, y_send.at[k], y_recv.at[k], up_id)

    def from_up(k):
        ref = rows(core, up, 1 - k) if k < 2 else rows(core, far, 1)
        return remote(ref, ref, y_send.at[3 + k], y_recv.at[3 + k], down_id)

    def mate_copy(n, src, of_y, h):
        return remote(src, rows(core, of_y, h), c_send.at[n], c_recv.at[n], mate_id)

    def from_mate(n, of_y, h):
        ref = rows(1 - core, of_y, h)
        return remote(ref, ref, c_send.at[n], c_recv.at[n], mate_id)

    for k in range(2):
        up_copy(k).start()
        down_copy(k).start()
    keep = pltpu.make_async_copy(items, table.at[core, pl.ds(y * held, held)], l_sem.at[0])
    keep.start()

    def start_z(k):
        to = (z + k) % n_z
        remote(message.at[to], msg_z.at[z], a_send.at[0], a_recv.at[0], at(x, to)).start()
        remote(ids.at[to], ids_z.at[z], a_send.at[1], a_recv.at[1], at(x, to)).start()

    def start_x(k):
        to = (x + k) % n_x
        remote(msg_z.at[:, to], msg_x.at[x], b_send.at[0], b_recv.at[0], at(to, z)).start()
        remote(ids_z.at[:, to], ids_x.at[x], b_send.at[1], b_recv.at[1], at(to, z)).start()

    z_done = [waiter(others(msg_z), a_send.at[0], a_recv.at[0]), waiter(others(ids_z), a_send.at[1], a_recv.at[1])]
    x_done = [waiter(others(msg_x), b_send.at[0], b_recv.at[0]), waiter(others(ids_x), b_send.at[1], b_recv.at[1])]

    each(n_z, start_z)
    for h in range(2):
        mate_copy(h, own(h), y, h).start()
    msg_z[z] = message[z]
    ids_z[z] = ids[z]

    from_down(0).wait_recv()
    up_copy(2).start()
    from_up(0).wait_recv()
    down_copy(2).start()
    mate_copy(2, rows(core, down, 0), down, 0).start()
    mate_copy(3, rows(core, up, 1), up, 1).start()

    for copy in z_done:
        copy.wait_recv()
    each(n_x, start_x)
    msg_x[x] = msg_z[:, x]
    ids_x[x] = ids_z[:, x]

    from_down(1).wait_recv()
    mate_copy(4, rows(core, down, 1), down, 1).start()
    from_up(1).wait_recv()
    mate_copy(5, rows(core, up, 0), up, 0).start()

    for copy in x_done:
        copy.wait_recv()
    to_smem = pltpu.make_async_copy(ids_x, ids_s, l_sem.at[1])
    to_smem.start()

    from_down(2).wait_recv()
    mate_copy(6, rows(core, far, 0), far, 0).start()
    from_up(2).wait_recv()
    mate_copy(7, rows(core, far, 1), far, 1).start()

    for copy in z_done + x_done:
        copy.wait_send()
    for k in range(3):
        up_copy(k).wait_send()
        down_copy(k).wait_send()
    halves = [(y, 0), (y, 1), (down, 0), (up, 1), (down, 1), (up, 0), (far, 0), (far, 1)]
    for n, (of_y, h) in enumerate(halves):
        mate_copy(n, rows(core, of_y, h), of_y, h).wait_send()
    for n, (of_y, h) in enumerate(halves):
        from_mate(n, of_y, h).wait_recv()
    keep.wait()
    to_smem.wait()

    hot_rows = [table[0, hot_id[0]], table[1, hot_id[1]]]
    row_of = lax.broadcasted_iota(i32, (16, 128), 0)
    masks = [((row_of == 6 + j) | (row_of == 9 + j)).astype(f32) for j in range(3)]

    def build(t, carry):
        xt, zt = t // n_z, t % n_z
        found = [table[s // CAP, ids_s[xt, zt, 0, s]] for s in range(2 * CAP)] + hot_rows
        chosen = jnp.concatenate(found, axis=0).T
        text = msg_x[xt, zt].astype(f32)
        scaled = []
        for u in range(2):
            weight = jnp.concatenate(
                [jnp.broadcast_to(text[3 * u + j:3 * u + j + 1], (128, 128)) for j in range(3)], axis=1)
            scaled.append(chosen * weight.astype(bf16))
        scaled = jnp.concatenate(scaled, axis=0)
        rating = jnp.concatenate([(text * masks[j]).astype(bf16) for j in range(3)], axis=1)
        left = jnp.concatenate([chosen, rating], axis=0)
        both = lax.dot_general(left, scaled, (((1,), (1,)), ((), ())), preferred_element_type=f32)
        for u in range(2):
            gram[2 * t + u] = both[:128, 128 * u:128 * u + 128]
            lot = both[128 + 6 + 3 * u:128 + 9 + 3 * u, 128 * u:128 * u + 128]
            part[ITERS, xt, zt, pl.ds(u, 1), :] = jnp.sum(lot, axis=0, keepdims=True)
        return carry

    lax.fori_loop(0, n_x * n_z, build, 0)

    def reduce(slot):
        def x_start(k):
            to = (x + k) % n_x
            remote(part.at[slot, to], red_x.at[slot, x], xs_sem.at[0, slot], xr_sem.at[0, slot], at(to, z)).start()

        def z_start(k):
            to = (z + k) % n_z
            remote(mid.at[slot, to], red_z.at[slot, z], zs_sem.at[0, slot], zr_sem.at[0, slot], at(x, to)).start()

        each(n_x, x_start)
        red_x[slot, x] = part[slot, x]
        reduced_x(slot).wait_recv()
        mid[slot] = jnp.sum(red_x[slot], axis=0)
        each(n_z, z_start)
        red_z[slot, z] = mid[slot, z]
        reduced_z(slot).wait_recv()
        return jnp.sum(red_z[slot], axis=0)

    def reduced_x(slot):
        return waiter(others(red_x, (slot,)), xs_sem.at[0, slot], xr_sem.at[0, slot])

    def reduced_z(slot):
        return waiter(others(red_z, (slot,)), zs_sem.at[0, slot], zr_sem.at[0, slot])

    def gather(slot, value):
        dir_z[slot, z] = value

        def z_start(k):
            own_dir = dir_z.at[slot, z]
            remote(own_dir, own_dir, zs_sem.at[1, slot], zr_sem.at[1, slot], at(x, (z + k) % n_z)).start()

        def x_start(k):
            remote(dir_z.at[slot], dir_x.at[slot, x], xs_sem.at[1, slot], xr_sem.at[1, slot], at((x + k) % n_x, z)).start()

        each(n_z, z_start)
        gathered_z(slot).wait_recv()
        each(n_x, x_start)
        dir_x[slot, x] = dir_z[slot]
        gathered_x(slot).wait_recv()

    def gathered_z(slot):
        return waiter(others(dir_z, (slot,)), zs_sem.at[1, slot], zr_sem.at[1, slot])

    def gathered_x(slot):
        return waiter(others(dir_x, (slot,)), xs_sem.at[1, slot], xr_sem.at[1, slot])

    group = min(4, n_z)

    def images(slot):
        def some(g, carry):
            xt, zt = g // (n_z // group), (g % (n_z // group)) * group
            lot = jnp.concatenate([dir_x[slot, xt, zt + i] for i in range(group)], axis=0)
            lot = lot.T
            for i in range(group):
                for u in range(2):
                    n = 2 * i + u
                    image = jnp.sum(gram[(xt * n_z + zt) * 2 + n] * lot[:, n:n + 1], axis=0, keepdims=True)
                    part[slot, xt, zt + i, pl.ds(u, 1), :] = image
            return carry

        lax.fori_loop(0, n_x * n_z // group, some, 0)

    right = reduce(ITERS)
    norm = jnp.sum(right * right, axis=-1, keepdims=True)

    def iterate(n, state):
        answer, residual, direction, norm = state
        gather(n, direction)
        images(n)
        image = reduce(n) + 0.1 * direction
        step = norm / jnp.sum(direction * image, axis=-1, keepdims=True)
        answer = answer + step * direction
        residual = residual - step * image
        after = jnp.sum(residual * residual, axis=-1, keepdims=True)
        direction = residual + (after / norm) * direction
        return answer, residual, direction, after

    state = lax.fori_loop(0, ITERS, iterate, (jnp.zeros_like(right), right, right, norm))
    out[...] = state[0]

    def sent(slot, carry):
        gathered_z(slot).wait_send()
        gathered_x(slot).wait_send()
        reduced_x(slot).wait_send()
        reduced_z(slot).wait_send()
        return carry

    lax.fori_loop(0, ITERS, sent, 0)
    reduced_x(ITERS).wait_send()
    reduced_z(ITERS).wait_send()


def body(n_x, n_z, ratings, confidence, rated, item_factors, cold_owner, cold_local, hot_group, hot_local):
    message, ids = prepare(n_x, n_z, ratings, confidence, rated, cold_owner, cold_local, hot_group)
    groups = lax.axis_index("dp") // 2 * 2 + jnp.arange(2, dtype=i32)
    hot_id = jnp.sum(jnp.where(hot_group[None, :] == groups[:, None], hot_local[None, :], 0), axis=1)
    users = confidence.shape[0]
    rows, width = item_factors.shape
    slots = ITERS + 1
    vmem = pl.BlockSpec(memory_space=pltpu.VMEM)
    smem = pl.BlockSpec(memory_space=pltpu.SMEM)
    dma = pltpu.SemaphoreType.DMA
    return pl.pallas_call(
        functools.partial(kernel, n_x, n_z),
        out_shape=jax.ShapeDtypeStruct((users, width), f32),
        in_specs=[vmem, vmem, pl.BlockSpec(memory_space=pl.ANY), smem],
        out_specs=vmem,
        scratch_shapes=[
            pltpu.VMEM((2, 4 * rows // BLK, BLK, width), bf16),
            pltpu.VMEM((n_z, n_x, 16, width), bf16),
            pltpu.VMEM((n_x, n_z, 16, width), bf16),
            pltpu.VMEM((n_z, n_x, 1, 128), i32),
            pltpu.VMEM((n_x, n_z, 1, 128), i32),
            pltpu.SMEM((n_x, n_z, 1, 128), i32),
            pltpu.VMEM((n_x * n_z * users, width, width), f32),
            pltpu.VMEM((slots, n_x, n_z, users, width), f32),
            pltpu.VMEM((slots, n_z, users, width), f32),
            pltpu.VMEM((slots, n_x, n_z, users, width), f32),
            pltpu.VMEM((slots, n_z, users, width), f32),
            pltpu.VMEM((slots, n_z, users, width), f32),
            pltpu.VMEM((slots, n_x, n_z, users, width), f32),
            dma((6,)), dma((6,)), dma((8,)), dma((8,)), dma((2,)),
            dma((2,)), dma((2,)), dma((2,)), dma((2,)),
            dma((2, slots)), dma((2, slots)), dma((2, slots)), dma((2, slots)),
        ],
        compiler_params=pltpu.CompilerParams(
            collective_id=0, has_side_effects=True, vmem_limit_bytes=40 * 1024 * 1024),
    )(message, ids, item_factors.reshape(-1, BLK, width), hot_id)


def solution(mesh):
    n_dp = mesh.shape["dp"]
    n_x = N_X
    n_z = n_dp // (2 * n_x)
    in_specs = (
        P(("dp", "rep"), None),
        P(("dp", "rep"), None),
        P(("dp", "rep"), None),
        P(("dp", "rep"), None),
        P("dp", "rep", None, None),
        P("dp", "rep", None),
        P(),
        P(),
    )
    return jax.shard_map(
        functools.partial(body, n_x, n_z), mesh=mesh, in_specs=in_specs,
        out_specs=P(("dp", "rep"), None), check_vma=False)
```

time: 534 us -> 160 us (0.30)
  waiting for transfers between devices: 357 us -> 0 us
  Pallas kernels: 0 us -> 151 us
  local copies, waits for them, and re-layouts: 56.4 us -> 6.32 us
  between operations: 33.5 us -> 0.27 us
  blocking collectives: 33 us -> 0 us
  matrix products: 24.6 us -> 0.44 us
  starting transfers between devices: 17.8 us -> 0 us
  other arithmetic: 9.7 us -> 0.94 us
    psum x1 -> x0, waiting for transfers between devices: 189 us -> none  [broadcast(): return lax.psum(kept, axis)]
    all_to_all x1 -> x0, waiting for transfers between devices: 159 us -> none  [body(): lax.all_to_all(served, 'dp', split_axis=0, concat_axis=0, tiled=True)]
    pallas_call x0 -> x1, Pallas kernels: none -> 151 us  [body(): pl.pallas_call(functools.partial(kernel, n_x, n_z), out_shape=jax.ShapeDt...]
    all_to_all x1 -> x0, blocking collectives: 33 us -> none  [body(): lax.all_to_all(wanted.reshape(dp_count, slot_count), 'dp', split_axis=0,...]
    dot_general x7 -> x2, matrix products: 24.6 us -> 0.44 us  [the longest x1 0.3 us: prepare(): jnp.dot(match.astype(bf16), both[:cold], preferred_element_type=f32)]
    all_to_all x1 -> x0, starting transfers between devices: 17.6 us -> none  [body(): lax.all_to_all(served, 'dp', split_axis=0, concat_axis=0, tiled=True)]
    gather x2 -> x0, local copies, waits for them, and re-layouts: 13.4 us -> none  [the longest x1 8.33 us: body(): cold_items = jnp.take(arrived, position, axis=0)]
    concatenate x1, local copies, waits for them, and re-layouts: 12.5 us -> 0.17 us  [prepare(): jnp.concatenate([cold_part, hot_part], axis=3)]
  transfers between devices with their start and end apart: 3 -> 0, of which waited for: 3 -> 0; matrix products, arithmetic and copies ran while one was open for 6% -> 0% of each run, Pallas kernels for 0% -> 0%
where the time goes in v1:
time: 160 us; the launch traced here: 159 us
  Pallas kernels  151 us (94%)
  local copies, waits for them, and re-layouts  6.32 us (4%)
    pallas_call x1, Pallas kernels, body(): pl.pallas_call(functools.partial(kernel, n_x, n_z), out_shape=jax.ShapeDt...  151 us
    unnamed x15, local copies, waits for them, and re-layouts  3.7 us

profile of v1, /device:TPU:6, one launch (start us, length us, event | category | flops | bytes accessed | tf_op | source)
XLA Modules:
  0.0 159.3 jit_solution(3719465332979995769)
XLA Ops:
  0.0 0.9 reshape.53
  1.0 0.1 reshape.52
  1.1 0.5 copy-done.4
  1.7 0.1 broadcast_multiply_fusion
  2.0 0.6 copy-done.3
  2.5 0.1 convolution_convert_fusion.1
  2.7 0.1 reshape.56
  2.9 0.1 reshape.57
  3.2 0.1 copy.25
  3.3 0.7 copy-done.2
  4.0 0.2 convert_reduce_fusion
  4.2 0.3 convolution_convert_fusion
  4.5 0.2 reshape.54
  4.6 0.1 copy.36
  4.8 0.1 reshape.55
  4.9 0.3 pad_maximum_fusion
  5.2 0.2 copy.30
  5.5 0.7 copy-done.5
  6.2 0.1 select_reduce_fusion
  6.4 0.1 reshape.59
  6.6 0.6 copy-done.6
  7.2 0.2 fusion.5.hot_id
  7.4 151.3 %shard_map.82 = f32[2,128]{1,0:T(2,128)S(1)} custom-call(bf16[16,4,16,128]{3,2,1,0:T(8,128)(2,1)S(1)} %pad.8.message, s32[16,4,1,128]{3,2,1,0:T(1,128)S(1)} %pad.9.ids, bf16[32,64,128]{2,1,0:T(8,128)(2,1)S(1)} %bitcast.20, s32[2]{0:T(128)S(1)} %fusion.5.hot_id), custom_call_target="tpu_custom_call" | custom-call | tf_op jit(solution)/shard_map/pallas_call | solution.py:316
  158.7 0.6 copy.40
  (23 shorter events, 0.6 us)
Async XLA Ops:
  0.0 1.0 copy-start.1
  1.0 0.7 copy-start.4
  1.9 0.7 copy-start.3
  3.3 0.7 copy-start.2
  5.4 2.0 %copy-start = (bf16[2048,128]{1,0:T(8,128)(2,1)S(1)}, bf16[2048,128]{1,0:T(8,128)(2,1)}, u32[]{:S(2)}) copy-start(bf16[2048,128]{1,0:T(8,128)(2,1)} %param.11) | copy-start | bytes 1572868
  5.5 0.7 copy-start.5
  6.6 0.7 copy-start.6

commit v2 on v1

--- a/solution.py
+++ b/solution.py
@@ -45,9 +45,10 @@
 
 
 def kernel(n_x, n_z, message, ids, items, hot_id, out,
-           table, msg_z, msg_x, ids_z, ids_x, ids_s, gram, part, mid, red_x, red_z, dir_z, dir_x,
-           y_send, y_recv, c_send, c_recv, l_sem,
-           a_send, a_recv, b_send, b_recv, zs_sem, zr_sem, xs_sem, xr_sem):
+           table, msg_z, msg_x, ids_z, ids_x, ids_s, one, two, one_x_half, one_x, one_z_half, one_z,
+           two_z_half, two_z, two_x_half, two_x,
+           y_send, y_recv, c_send, c_recv, l_sem, a_send, a_recv, b_send, b_recv,
+           one_x_sem, one_z_sem, two_z_sem, two_x_sem):
     dp = lax.axis_index("dp")
     y = lax.axis_index("rep")
     core = dp % 2
@@ -188,9 +189,20 @@
     hot_rows = [table[0, hot_id[0]], table[1, hot_id[1]]]
     row_of = lax.broadcasted_iota(i32, (16, 128), 0)
     masks = [((row_of == 6 + j) | (row_of == 9 + j)).astype(f32) for j in range(3)]
+    lane_block = lax.broadcasted_iota(i32, (8, 128), 1) // 8
+    window = [(lane_block >= i) & (lane_block < i + 8) for i in range(8)]
+
+    def x_at(p):
+        return (x + jnp.where(p == 0, 2, jnp.where(p == 1, 1, jnp.where(p == 2, 3, 0)))) % n_x
+
+    def z_at(place):
+        ahead = n_z // 2 - (place + 1) // 2
+        behind = n_z // 2 + place // 2
+        return (z + jnp.where(place % 2 == 1, ahead, behind)) % n_z
 
     def build(t, carry):
-        xt, zt = t // n_z, t % n_z
+        p, place = t // n_z, t % n_z
+        xt, zt = x_at(p), z_at(place)
         found = [table[s // CAP, ids_s[xt, zt, 0, s]] for s in range(2 * CAP)] + hot_rows
         chosen = jnp.concatenate(found, axis=0).T
         text = msg_x[xt, zt].astype(f32)
@@ -203,84 +215,171 @@
         rating = jnp.concatenate([(text * masks[j]).astype(bf16) for j in range(3)], axis=1)
         left = jnp.concatenate([chosen, rating], axis=0)
         both = lax.dot_general(left, scaled, (((1,), (1,)), ((), ())), preferred_element_type=f32)
-        for u in range(2):
-            gram[2 * t + u] = both[:128, 128 * u:128 * u + 128]
-            lot = both[128 + 6 + 3 * u:128 + 9 + 3 * u, 128 * u:128 * u + 128]
-            part[ITERS, xt, zt, pl.ds(u, 1), :] = jnp.sum(lot, axis=0, keepdims=True)
+
+        def group(u, i):
+            return both[8 * i:8 * i + 8, 128 * u:128 * u + 128]
+
+        main = [[jnp.where(window[i], group(u, i), group(u, i + 8)) for i in range(8)] for u in range(2)]
+        shared = group(0, 0)
+        for i in range(8):
+            shared = jnp.where(lane_block == i + 8, group(0, i), shared)
+            shared = jnp.where(lane_block == i, group(1, i + 8), shared)
+        right = [
+            jnp.sum(both[134 + 3 * u:137 + 3 * u, 128 * u:128 * u + 128], axis=0, keepdims=True)
+            for u in range(2)
+        ]
+        one[p, place] = jnp.concatenate(main[0], axis=0)
+        two[p, place] = jnp.concatenate(main[1] + [shared] + right + [jnp.zeros((6, 128), f32)], axis=0)
         return carry
 
     lax.fori_loop(0, n_x * n_z, build, 0)
 
-    def reduce(slot):
-        def x_start(k):
-            to = (x + k) % n_x
-            remote(part.at[slot, to], red_x.at[slot, x], xs_sem.at[0, slot], xr_sem.at[0, slot], at(to, z)).start()
-
-        def z_start(k):
-            to = (z + k) % n_z
-            remote(mid.at[slot, to], red_z.at[slot, z], zs_sem.at[0, slot], zr_sem.at[0, slot], at(x, to)).start()
-
-        each(n_x, x_start)
-        red_x[slot, x] = part[slot, x]
-        reduced_x(slot).wait_recv()
-        mid[slot] = jnp.sum(red_x[slot], axis=0)
-        each(n_z, z_start)
-        red_z[slot, z] = mid[slot, z]
-        reduced_z(slot).wait_recv()
-        return jnp.sum(red_z[slot], axis=0)
-
-    def reduced_x(slot):
-        return waiter(others(red_x, (slot,)), xs_sem.at[0, slot], xr_sem.at[0, slot])
-
-    def reduced_z(slot):
-        return waiter(others(red_z, (slot,)), zs_sem.at[0, slot], zr_sem.at[0, slot])
-
-    def gather(slot, value):
-        dir_z[slot, z] = value
-
-        def z_start(k):
-            own_dir = dir_z.at[slot, z]
-            remote(own_dir, own_dir, zs_sem.at[1, slot], zr_sem.at[1, slot], at(x, (z + k) % n_z)).start()
-
-        def x_start(k):
-            remote(dir_z.at[slot], dir_x.at[slot, x], xs_sem.at[1, slot], xr_sem.at[1, slot], at((x + k) % n_x, z)).start()
-
-        each(n_z, z_start)
-        gathered_z(slot).wait_recv()
-        each(n_x, x_start)
-        dir_x[slot, x] = dir_z[slot]
-        gathered_x(slot).wait_recv()
-
-    def gathered_z(slot):
-        return waiter(others(dir_z, (slot,)), zs_sem.at[1, slot], zr_sem.at[1, slot])
-
-    def gathered_x(slot):
-        return waiter(others(dir_x, (slot,)), xs_sem.at[1, slot], xr_sem.at[1, slot])
-
-    group = min(4, n_z)
-
-    def images(slot):
-        def some(g, carry):
-            xt, zt = g // (n_z // group), (g % (n_z // group)) * group
-            lot = jnp.concatenate([dir_x[slot, xt, zt + i] for i in range(group)], axis=0)
-            lot = lot.T
-            for i in range(group):
-                for u in range(2):
-                    n = 2 * i + u
-                    image = jnp.sum(gram[(xt * n_z + zt) * 2 + n] * lot[:, n:n + 1], axis=0, keepdims=True)
-                    part[slot, xt, zt + i, pl.ds(u, 1), :] = image
-            return carry
-
-        lax.fori_loop(0, n_x * n_z // group, some, 0)
-
-    right = reduce(ITERS)
-    norm = jnp.sum(right * right, axis=-1, keepdims=True)
+    last_x, last_z = n_x - 1, n_z - 1
+    to_x = (at((x + 1) % n_x, z), at((x + n_x - 1) % n_x, z))
+    to_z = (at(x, (z + 1) % n_z), at(x, (z + n_z - 1) % n_z))
+    quarter = n_z // 4
+    one_rows, two_rows = one.shape[2] // 2, two.shape[2] // 2
+    steps_x, steps_z = n_x // 2, n_z // 2
+
+    def place(way, step, steps):
+        if step == steps:
+            return 2 * steps - 1
+        return 0 if step == 0 else 2 * step - 1 + way
+
+    def one_x_copy(way, step, j):
+        lots = pl.ds(quarter * j, quarter)
+        sems = one_x_sem.at[0, way, step, j], one_x_sem.at[1, way, step, j]
+        if step == 0:
+            return remote(one.at[0, lots, pl.ds(one_rows * way, one_rows)], one_x_half.at[way, lots], *sems, to_x[way])
+        return remote(one.at[place(way, step, steps_x), lots], one_x.at[way, step - 1, lots], *sems, to_x[way])
+
+    def one_z_copy(way, step):
+        sems = one_z_sem.at[0, way, step], one_z_sem.at[1, way, step]
+        if step == 0:
+            return remote(one.at[last_x, 0, pl.ds(one_rows * way, one_rows)], one_z_half.at[way], *sems, to_z[way])
+        return remote(one.at[last_x, place(way, step, steps_z)], one_z.at[way, step - 1], *sems, to_z[way])
+
+    def two_z_copy(way, step, p):
+        sems = two_z_sem.at[0, way, step, p], two_z_sem.at[1, way, step, p]
+        if step == 0:
+            return remote(two.at[p, 0, pl.ds(two_rows * way, two_rows)], two_z_half.at[way, p], *sems, to_z[way])
+        return remote(two.at[p, place(way, step, steps_z)], two_z.at[way, step - 1, p], *sems, to_z[way])
+
+    def two_x_copy(way, step):
+        sems = two_x_sem.at[0, way, step], two_x_sem.at[1, way, step]
+        if step == 0:
+            return remote(two.at[0, last_z, pl.ds(two_rows * way, two_rows)], two_x_half.at[way], *sems, to_x[way])
+        return remote(two.at[place(way, step, steps_x), last_z], two_x.at[way, step - 1], *sems, to_x[way])
+
+    def one_x_event(step, j):
+        for way in range(2):
+            one_x_copy(way, step, j).wait_recv()
+            lots = pl.ds(quarter * j, quarter)
+            at_place = place(way, step + 1, steps_x)
+            if step == 0:
+                one[at_place, lots, pl.ds(one_rows * way, one_rows)] += one_x_half[way, lots]
+            else:
+                one[at_place, lots] += one_x[way, step - 1, lots]
+            if step + 1 < steps_x:
+                one_x_copy(way, step + 1, j).start()
+
+    def one_z_event(step):
+        for way in range(2):
+            one_z_copy(way, step).wait_recv()
+            at_place = place(way, step + 1, steps_z)
+            if step == 0:
+                one[last_x, at_place, pl.ds(one_rows * way, one_rows)] += one_z_half[way]
+            else:
+                one[last_x, at_place] += one_z[way, step - 1]
+            if step + 1 < steps_z:
+                one_z_copy(way, step + 1).start()
+
+    def two_z_event(step, p):
+        for way in range(2):
+            two_z_copy(way, step, p).wait_recv()
+            at_place = place(way, step + 1, steps_z)
+            if step == 0:
+                two[p, at_place, pl.ds(two_rows * way, two_rows)] += two_z_half[way, p]
+            else:
+                two[p, at_place] += two_z[way, step - 1, p]
+            if step + 1 < steps_z:
+                two_z_copy(way, step + 1, p).start()
+
+    def two_x_event(step):
+        for way in range(2):
+            two_x_copy(way, step).wait_recv()
+            at_place = place(way, step + 1, steps_x)
+            if step == 0:
+                two[at_place, last_z, pl.ds(two_rows * way, two_rows)] += two_x_half[way]
+            else:
+                two[at_place, last_z] += two_x[way, step - 1]
+            if step + 1 < steps_x:
+                two_x_copy(way, step + 1).start()
+
+    delay = 2.5
+    one_unit, two_unit = 2.6, 0.82
+    events = []
+    for step in range(steps_x):
+        for j in range(4):
+            begun = 4 * one_unit * (step - 0.5) if step else 0.0
+            events.append((delay + begun + one_unit * (j + 1) * (1 if step else 0.5), one_x_event, (step, j)))
+    ready = [when for when, _, args in events if args[0] == steps_x - 1]
+
+    def one_z_first():
+        for way in range(2):
+            one_z_copy(way, 0).start()
+
+    def two_x_first():
+        for way in range(2):
+            two_x_copy(way, 0).start()
+
+    when = ready[0] + 0.01
+    events.append((when, one_z_first, ()))
+    for step in range(steps_z):
+        needed = max(place(way, step + 1, steps_z) for way in range(2)) // quarter
+        when = max(when + 3.0, ready[needed] + 0.02)
+        events.append((when, one_z_event, (step,)))
+    for step in range(steps_z):
+        for p in range(n_x):
+            begun = 4 * two_unit * (step - 0.5) if step else 0.0
+            when = delay + begun + two_unit * (p + 1) * (1 if step else 0.5)
+            events.append((when, two_z_event, (step, p)))
+    when += 0.01
+    events.append((when, two_x_first, ()))
+    for step in range(steps_x):
+        when += 3.0
+        events.append((when, two_x_event, (step,)))
+
+    for j in range(4):
+        for way in range(2):
+            one_x_copy(way, 0, j).start()
+            two_z_copy(way, 0, j).start()
+    for _, event, args in sorted(events, key=lambda entry: entry[0]):
+        event(*args)
+
+    row_block = lax.broadcasted_iota(i32, (128, 128), 0) // 8
+    own_block = row_block == lax.broadcasted_iota(i32, (128, 128), 1) // 8
+    lot = two[last_x, last_z]
+    grams = []
+    for u in range(2):
+        main = one[last_x, last_z] if u == 0 else lot[:64]
+        upper = [jnp.where(window[i], main[8 * i:8 * i + 8], 0.0) for i in range(8)]
+        lower = [jnp.where(window[i], 0.0, main[8 * i:8 * i + 8]) for i in range(8)]
+        for i in range(8):
+            if u == 0:
+                upper[i] = jnp.where(lane_block == i + 8, lot[64:72], upper[i])
+            else:
+                lower[i] = jnp.where(lane_block == i, lot[64:72], lower[i])
+        kept = jnp.concatenate(upper + lower, axis=0)
+        grams.append(kept + jnp.where(own_block, 0.0, kept).T)
+    right = lot[72:74]
 
     def iterate(n, state):
         answer, residual, direction, norm = state
-        gather(n, direction)
-        images(n)
-        image = reduce(n) + 0.1 * direction
+        turned = jnp.concatenate([direction, jnp.zeros((6, 128), f32)], axis=0).T
+        image = jnp.concatenate(
+            [jnp.sum(grams[u] * turned[:, u:u + 1], axis=0, keepdims=True) for u in range(2)], axis=0)
+        image = image + 0.1 * direction
         step = norm / jnp.sum(direction * image, axis=-1, keepdims=True)
         answer = answer + step * direction
         residual = residual - step * image
@@ -288,19 +387,20 @@
         direction = residual + (after / norm) * direction
         return answer, residual, direction, after
 
-    state = lax.fori_loop(0, ITERS, iterate, (jnp.zeros_like(right), right, right, norm))
+    state = (jnp.zeros_like(right), right, right, jnp.sum(right * right, axis=-1, keepdims=True))
+    for n in range(ITERS):
+        state = iterate(n, state)
     out[...] = state[0]
 
-    def sent(slot, carry):
-        gathered_z(slot).wait_send()
-        gathered_x(slot).wait_send()
-        reduced_x(slot).wait_send()
-        reduced_z(slot).wait_send()
-        return carry
-
-    lax.fori_loop(0, ITERS, sent, 0)
-    reduced_x(ITERS).wait_send()
-    reduced_z(ITERS).wait_send()
+    for way in range(2):
+        for step in range(steps_x):
+            two_x_copy(way, step).wait_send()
+            for j in range(4):
+                one_x_copy(way, step, j).wait_send()
+        for step in range(steps_z):
+            one_z_copy(way, step).wait_send()
+            for p in range(n_x):
+                two_z_copy(way, step, p).wait_send()
 
 
 def body(n_x, n_z, ratings, confidence, rated, item_factors, cold_owner, cold_local, hot_group, hot_local):
@@ -309,7 +409,6 @@
     hot_id = jnp.sum(jnp.where(hot_group[None, :] == groups[:, None], hot_local[None, :], 0), axis=1)
     users = confidence.shape[0]
     rows, width = item_factors.shape
-    slots = ITERS + 1
     vmem = pl.BlockSpec(memory_space=pltpu.VMEM)
     smem = pl.BlockSpec(memory_space=pltpu.SMEM)
     dma = pltpu.SemaphoreType.DMA
@@ -325,16 +424,19 @@
             pltpu.VMEM((n_z, n_x, 1, 128), i32),
             pltpu.VMEM((n_x, n_z, 1, 128), i32),
             pltpu.SMEM((n_x, n_z, 1, 128), i32),
-            pltpu.VMEM((n_x * n_z * users, width, width), f32),
-            pltpu.VMEM((slots, n_x, n_z, users, width), f32),
-            pltpu.VMEM((slots, n_z, users, width), f32),
-            pltpu.VMEM((slots, n_x, n_z, users, width), f32),
-            pltpu.VMEM((slots, n_z, users, width), f32),
-            pltpu.VMEM((slots, n_z, users, width), f32),
-            pltpu.VMEM((slots, n_x, n_z, users, width), f32),
+            pltpu.VMEM((n_x, n_z, 64, width), f32),
+            pltpu.VMEM((n_x, n_z, 80, width), f32),
+            pltpu.VMEM((2, n_z, 32, width), f32),
+            pltpu.VMEM((2, n_x // 2 - 1, n_z, 64, width), f32),
+            pltpu.VMEM((2, 32, width), f32),
+            pltpu.VMEM((2, n_z // 2 - 1, 64, width), f32),
+            pltpu.VMEM((2, n_x, 40, width), f32),
+            pltpu.VMEM((2, n_z // 2 - 1, n_x, 80, width), f32),
+            pltpu.VMEM((2, 40, width), f32),
+            pltpu.VMEM((2, n_x // 2 - 1, 80, width), f32),
             dma((6,)), dma((6,)), dma((8,)), dma((8,)), dma((2,)),
             dma((2,)), dma((2,)), dma((2,)), dma((2,)),
-            dma((2, slots)), dma((2, slots)), dma((2, slots)), dma((2, slots)),
+            dma((2, 2, n_x // 2, 4)), dma((2, 2, n_z // 2)), dma((2, 2, n_z // 2, n_x)), dma((2, 2, n_x // 2)),
         ],
         compiler_params=pltpu.CompilerParams(
             collective_id=0, has_side_effects=True, vmem_limit_bytes=40 * 1024 * 1024),

time: 160 us -> 113 us (0.71)
  the two profiles are of different devices: /device:TPU:6 before, /device:TPU:24 now
where the time goes in v2:
time: 113 us
  Pallas kernels  105 us (93%)
  local copies, waits for them, and re-layouts  6.32 us (6%)
    pallas_call x1, Pallas kernels, body(): pl.pallas_call(functools.partial(kernel, n_x, n_z), out_shape=jax.ShapeDt...  105 us
    unnamed x15, local copies, waits for them, and re-layouts  3.7 us

profile of v2, /device:TPU:24, one launch (start us, length us, event | category | flops | bytes accessed | tf_op | source)
XLA Modules:
  0.0 112.6 jit_solution(2557152921262293325)
XLA Ops:
  0.0 0.9 reshape.53
  1.0 0.1 reshape.52
  1.1 0.5 copy-done.4
  1.7 0.1 broadcast_multiply_fusion
  2.0 0.6 copy-done.3
  2.5 0.1 convolution_convert_fusion.1
  2.7 0.1 reshape.56
  2.9 0.1 reshape.57
  3.2 0.1 copy.25
  3.3 0.7 copy-done.2
  4.0 0.2 convert_reduce_fusion
  4.2 0.3 convolution_convert_fusion
  4.5 0.2 reshape.54
  4.6 0.1 copy.36
  4.8 0.1 reshape.55
  4.9 0.3 pad_maximum_fusion
  5.2 0.2 copy.30
  5.5 0.7 copy-done.5
  6.2 0.1 select_reduce_fusion
  6.4 0.1 reshape.59
  6.6 0.6 copy-done.6
  7.2 0.2 fusion.5.hot_id
  7.4 104.7 %shard_map.82 = f32[2,128]{1,0:T(2,128)S(1)} custom-call(bf16[16,4,16,128]{3,2,1,0:T(8,128)(2,1)S(1)} %pad.8.message, s32[16,4,1,128]{3,2,1,0:T(1,128)S(1)} %pad.9.ids, bf16[32,64,128]{2,1,0:T(8,128)(2,1)S(1)} %bitcast.20, s32[2]{0:T(128)S(1)} %fusion.5.hot_id), custom_call_target="tpu_custom_call" | custom-call | tf_op jit(solution)/shard_map/pallas_call | solution.py:415
  112.1 0.6 copy.40
  (23 shorter events, 0.6 us)
Async XLA Ops:
  0.0 1.0 copy-start.1
  1.0 0.7 copy-start.4
  1.9 0.7 copy-start.3
  3.3 0.7 copy-start.2
  5.4 2.0 %copy-start = (bf16[2048,128]{1,0:T(8,128)(2,1)S(1)}, bf16[2048,128]{1,0:T(8,128)(2,1)}, u32[]{:S(2)}) copy-start(bf16[2048,128]{1,0:T(8,128)(2,1)} %param.11) | copy-start | bytes 1572868
  5.5 0.7 copy-start.5
  6.6 0.7 copy-start.6

commit v3 on v2

--- a/solution.py
+++ b/solution.py
@@ -11,6 +11,11 @@
 CAP = 2
 ITERS = 3
 N_X = 4
+PACKED_ROWS = 144
+ONE_ROWS = 80
+TWO_ROWS = PACKED_ROWS - ONE_ROWS
+LOTS_X = 4
+LOTS_Z = 4
 MESH = pl.DeviceIdType.MESH
 bf16, f32, i32 = jnp.bfloat16, jnp.float32, jnp.int32
 
@@ -192,17 +197,18 @@
     lane_block = lax.broadcasted_iota(i32, (8, 128), 1) // 8
     window = [(lane_block >= i) & (lane_block < i + 8) for i in range(8)]
 
-    def x_at(p):
-        return (x + jnp.where(p == 0, 2, jnp.where(p == 1, 1, jnp.where(p == 2, 3, 0)))) % n_x
-
     def z_at(place):
         ahead = n_z // 2 - (place + 1) // 2
         behind = n_z // 2 + place // 2
         return (z + jnp.where(place % 2 == 1, ahead, behind)) % n_z
 
-    def build(t, carry):
-        p, place = t // n_z, t % n_z
-        xt, zt = x_at(p), z_at(place)
+    def build(place, carry):
+        for p in range(n_x):
+            build_one(p, place)
+        return carry
+
+    def build_one(p, place):
+        xt, zt = (x + (2, 1, 3, 0)[p]) % n_x, z_at(place)
         found = [table[s // CAP, ids_s[xt, zt, 0, s]] for s in range(2 * CAP)] + hot_rows
         chosen = jnp.concatenate(found, axis=0).T
         text = msg_x[xt, zt].astype(f32)
@@ -228,16 +234,15 @@
             jnp.sum(both[134 + 3 * u:137 + 3 * u, 128 * u:128 * u + 128], axis=0, keepdims=True)
             for u in range(2)
         ]
-        one[p, place] = jnp.concatenate(main[0], axis=0)
-        two[p, place] = jnp.concatenate(main[1] + [shared] + right + [jnp.zeros((6, 128), f32)], axis=0)
-        return carry
-
-    lax.fori_loop(0, n_x * n_z, build, 0)
+        packed = main[0] + main[1] + [shared, jnp.concatenate(right + [jnp.zeros((6, 128), f32)], axis=0)]
+        one[p, place] = jnp.concatenate(packed[:one.shape[2] // 8], axis=0)
+        two[p, place] = jnp.concatenate(packed[one.shape[2] // 8:], axis=0)
 
     last_x, last_z = n_x - 1, n_z - 1
     to_x = (at((x + 1) % n_x, z), at((x + n_x - 1) % n_x, z))
     to_z = (at(x, (z + 1) % n_z), at(x, (z + n_z - 1) % n_z))
-    quarter = n_z // 4
+    quarter = n_z // LOTS_X
+    wide = n_x // LOTS_Z
     one_rows, two_rows = one.shape[2] // 2, two.shape[2] // 2
     steps_x, steps_z = n_x // 2, n_z // 2
 
@@ -261,9 +266,10 @@
 
     def two_z_copy(way, step, p):
         sems = two_z_sem.at[0, way, step, p], two_z_sem.at[1, way, step, p]
+        lot = pl.ds(p * wide, wide)
         if step == 0:
-            return remote(two.at[p, 0, pl.ds(two_rows * way, two_rows)], two_z_half.at[way, p], *sems, to_z[way])
-        return remote(two.at[p, place(way, step, steps_z)], two_z.at[way, step - 1, p], *sems, to_z[way])
+            return remote(two.at[lot, 0, pl.ds(two_rows * way, two_rows)], two_z_half.at[way, lot], *sems, to_z[way])
+        return remote(two.at[lot, place(way, step, steps_z)], two_z.at[way, step - 1, lot], *sems, to_z[way])
 
     def two_x_copy(way, step):
         sems = two_x_sem.at[0, way, step], two_x_sem.at[1, way, step]
@@ -271,108 +277,134 @@
             return remote(two.at[0, last_z, pl.ds(two_rows * way, two_rows)], two_x_half.at[way], *sems, to_x[way])
         return remote(two.at[place(way, step, steps_x), last_z], two_x.at[way, step - 1], *sems, to_x[way])
 
+    delay, event_us, build_us = 2.5, 0.15, 0.5
+    clock = {"now": 0.0, "x": 0.0, "z": 0.0}
+    built, serial, pending, done_x, done_z = [0], [0], [], [], []
+
+    def sent(axis, rows_sent, event, args):
+        clock[axis] = max(clock[axis], clock["now"]) + rows_sent * 2 * 512 / 1e5
+        serial[0] += 1
+        pending.append((clock[axis] + delay, serial[0], event, args))
+
+    def start_one_x(step, j):
+        for way in range(2):
+            one_x_copy(way, step, j).start()
+        sent("x", quarter * one_rows * (2 if step else 1), one_x_event, (step, j))
+
+    def start_one_z(step):
+        for way in range(2):
+            one_z_copy(way, step).start()
+        sent("z", one_rows * (2 if step else 1), one_z_event, (step,))
+
+    def start_two_z(step, p):
+        for way in range(2):
+            two_z_copy(way, step, p).start()
+        sent("z", wide * two_rows * (2 if step else 1), two_z_event, (step, p))
+
+    def start_two_x(step):
+        for way in range(2):
+            two_x_copy(way, step).start()
+        sent("x", two_rows * (2 if step else 1), two_x_event, (step,))
+
+    def ready_one_z():
+        step = len(done_z)
+        needed = max(place(way, step, steps_z) for way in range(2)) // quarter
+        if step < steps_z and needed in done_x and ("one", step) not in begun:
+            begun.add(("one", step))
+            start_one_z(step)
+
+    begun = set()
+
     def one_x_event(step, j):
         for way in range(2):
-            one_x_copy(way, step, j).wait_recv()
+            one_x_copy(way, step, j).wait()
             lots = pl.ds(quarter * j, quarter)
             at_place = place(way, step + 1, steps_x)
             if step == 0:
                 one[at_place, lots, pl.ds(one_rows * way, one_rows)] += one_x_half[way, lots]
             else:
                 one[at_place, lots] += one_x[way, step - 1, lots]
-            if step + 1 < steps_x:
-                one_x_copy(way, step + 1, j).start()
+        if step + 1 < steps_x:
+            start_one_x(step + 1, j)
+        else:
+            done_x.append(j)
+            ready_one_z()
 
     def one_z_event(step):
         for way in range(2):
-            one_z_copy(way, step).wait_recv()
+            one_z_copy(way, step).wait()
             at_place = place(way, step + 1, steps_z)
             if step == 0:
                 one[last_x, at_place, pl.ds(one_rows * way, one_rows)] += one_z_half[way]
             else:
                 one[last_x, at_place] += one_z[way, step - 1]
-            if step + 1 < steps_z:
-                one_z_copy(way, step + 1).start()
+        done_z.append(step)
+        ready_one_z()
 
     def two_z_event(step, p):
-        for way in range(2):
-            two_z_copy(way, step, p).wait_recv()
+        lot = pl.ds(p * wide, wide)
+        for way in range(2):
+            two_z_copy(way, step, p).wait()
             at_place = place(way, step + 1, steps_z)
+            while at_place >= built[0]:
+                build_some()
             if step == 0:
-                two[p, at_place, pl.ds(two_rows * way, two_rows)] += two_z_half[way, p]
+                two[lot, at_place, pl.ds(two_rows * way, two_rows)] += two_z_half[way, lot]
             else:
-                two[p, at_place] += two_z[way, step - 1, p]
-            if step + 1 < steps_z:
-                two_z_copy(way, step + 1, p).start()
+                two[lot, at_place] += two_z[way, step - 1, lot]
+        if step + 1 < steps_z:
+            start_two_z(step + 1, p)
+        elif p == n_x // wide - 1:
+            start_two_x(0)
 
     def two_x_event(step):
         for way in range(2):
-            two_x_copy(way, step).wait_recv()
+            two_x_copy(way, step).wait()
             at_place = place(way, step + 1, steps_x)
             if step == 0:
                 two[at_place, last_z, pl.ds(two_rows * way, two_rows)] += two_x_half[way]
             else:
                 two[at_place, last_z] += two_x[way, step - 1]
-            if step + 1 < steps_x:
-                two_x_copy(way, step + 1).start()
-
-    delay = 2.5
-    one_unit, two_unit = 2.6, 0.82
-    events = []
-    for step in range(steps_x):
-        for j in range(4):
-            begun = 4 * one_unit * (step - 0.5) if step else 0.0
-            events.append((delay + begun + one_unit * (j + 1) * (1 if step else 0.5), one_x_event, (step, j)))
-    ready = [when for when, _, args in events if args[0] == steps_x - 1]
-
-    def one_z_first():
-        for way in range(2):
-            one_z_copy(way, 0).start()
-
-    def two_x_first():
-        for way in range(2):
-            two_x_copy(way, 0).start()
-
-    when = ready[0] + 0.01
-    events.append((when, one_z_first, ()))
-    for step in range(steps_z):
-        needed = max(place(way, step + 1, steps_z) for way in range(2)) // quarter
-        when = max(when + 3.0, ready[needed] + 0.02)
-        events.append((when, one_z_event, (step,)))
-    for step in range(steps_z):
-        for p in range(n_x):
-            begun = 4 * two_unit * (step - 0.5) if step else 0.0
-            when = delay + begun + two_unit * (p + 1) * (1 if step else 0.5)
-            events.append((when, two_z_event, (step, p)))
-    when += 0.01
-    events.append((when, two_x_first, ()))
-    for step in range(steps_x):
-        when += 3.0
-        events.append((when, two_x_event, (step,)))
-
-    for j in range(4):
-        for way in range(2):
-            one_x_copy(way, 0, j).start()
-            two_z_copy(way, 0, j).start()
-    for _, event, args in sorted(events, key=lambda entry: entry[0]):
+        if step + 1 < steps_x:
+            start_two_x(step + 1)
+
+    def build_some():
+        first = built[0]
+        size = 1 if first == 0 else n_z // 4 - first % (n_z // 4)
+        lax.fori_loop(first, first + size, build, 0)
+        built[0] += size
+        clock["now"] += build_us * size
+        if first == 0:
+            for p in range(n_x // wide):
+                start_two_z(0, p)
+        if built[0] % quarter == 0:
+            start_one_x(0, built[0] // quarter - 1)
+
+    while pending or built[0] < n_z:
+        pending.sort()
+        if built[0] < n_z and not (pending and pending[0][0] <= clock["now"]):
+            build_some()
+            continue
+        arrival, _, event, args = pending.pop(0)
+        clock["now"] = max(clock["now"], arrival) + event_us
         event(*args)
 
     row_block = lax.broadcasted_iota(i32, (128, 128), 0) // 8
     own_block = row_block == lax.broadcasted_iota(i32, (128, 128), 1) // 8
-    lot = two[last_x, last_z]
+    lot = jnp.concatenate([one[last_x, last_z], two[last_x, last_z]], axis=0)
     grams = []
     for u in range(2):
-        main = one[last_x, last_z] if u == 0 else lot[:64]
+        main = lot[64 * u:64 * u + 64]
         upper = [jnp.where(window[i], main[8 * i:8 * i + 8], 0.0) for i in range(8)]
         lower = [jnp.where(window[i], 0.0, main[8 * i:8 * i + 8]) for i in range(8)]
         for i in range(8):
             if u == 0:
-                upper[i] = jnp.where(lane_block == i + 8, lot[64:72], upper[i])
+                upper[i] = jnp.where(lane_block == i + 8, lot[128:136], upper[i])
             else:
-                lower[i] = jnp.where(lane_block == i, lot[64:72], lower[i])
+                lower[i] = jnp.where(lane_block == i, lot[128:136], lower[i])
         kept = jnp.concatenate(upper + lower, axis=0)
         grams.append(kept + jnp.where(own_block, 0.0, kept).T)
-    right = lot[72:74]
+    right = lot[136:138]
 
     def iterate(n, state):
         answer, residual, direction, norm = state
@@ -391,16 +423,6 @@
     for n in range(ITERS):
         state = iterate(n, state)
     out[...] = state[0]
-
-    for way in range(2):
-        for step in range(steps_x):
-            two_x_copy(way, step).wait_send()
-            for j in range(4):
-                one_x_copy(way, step, j).wait_send()
-        for step in range(steps_z):
-            one_z_copy(way, step).wait_send()
-            for p in range(n_x):
-                two_z_copy(way, step, p).wait_send()
 
 
 def body(n_x, n_z, ratings, confidence, rated, item_factors, cold_owner, cold_local, hot_group, hot_local):
@@ -424,19 +446,19 @@
             pltpu.VMEM((n_z, n_x, 1, 128), i32),
             pltpu.VMEM((n_x, n_z, 1, 128), i32),
             pltpu.SMEM((n_x, n_z, 1, 128), i32),
-            pltpu.VMEM((n_x, n_z, 64, width), f32),
-            pltpu.VMEM((n_x, n_z, 80, width), f32),
-            pltpu.VMEM((2, n_z, 32, width), f32),
-            pltpu.VMEM((2, n_x // 2 - 1, n_z, 64, width), f32),
-            pltpu.VMEM((2, 32, width), f32),
-            pltpu.VMEM((2, n_z // 2 - 1, 64, width), f32),
-            pltpu.VMEM((2, n_x, 40, width), f32),
-            pltpu.VMEM((2, n_z // 2 - 1, n_x, 80, width), f32),
-            pltpu.VMEM((2, 40, width), f32),
-            pltpu.VMEM((2, n_x // 2 - 1, 80, width), f32),
+            pltpu.VMEM((n_x, n_z, ONE_ROWS, width), f32),
+            pltpu.VMEM((n_x, n_z, TWO_ROWS, width), f32),
+            pltpu.VMEM((2, n_z, ONE_ROWS // 2, width), f32),
+            pltpu.VMEM((2, n_x // 2 - 1, n_z, ONE_ROWS, width), f32),
+            pltpu.VMEM((2, ONE_ROWS // 2, width), f32),
+            pltpu.VMEM((2, n_z // 2 - 1, ONE_ROWS, width), f32),
+            pltpu.VMEM((2, n_x, TWO_ROWS // 2, width), f32),
+            pltpu.VMEM((2, n_z // 2 - 1, n_x, TWO_ROWS, width), f32),
+            pltpu.VMEM((2, TWO_ROWS // 2, width), f32),
+            pltpu.VMEM((2, n_x // 2 - 1, TWO_ROWS, width), f32),
             dma((6,)), dma((6,)), dma((8,)), dma((8,)), dma((2,)),
             dma((2,)), dma((2,)), dma((2,)), dma((2,)),
-            dma((2, 2, n_x // 2, 4)), dma((2, 2, n_z // 2)), dma((2, 2, n_z // 2, n_x)), dma((2, 2, n_x // 2)),
+            dma((2, 2, n_x // 2, LOTS_X)), dma((2, 2, n_z // 2)), dma((2, 2, n_z // 2, LOTS_Z)), dma((2, 2, n_x // 2)),
         ],
         compiler_params=pltpu.CompilerParams(
             collective_id=0, has_side_effects=True, vmem_limit_bytes=40 * 1024 * 1024),

time: 113 us -> 94.7 us (0.84)
  the two profiles are of different devices: /device:TPU:24 before, /device:TPU:6 now
where the time goes in v3:
time: 94.7 us; the launch traced here: 93.3 us
  Pallas kernels  85.3 us (90%)
  local copies, waits for them, and re-layouts  6.32 us (7%)
    pallas_call x1, Pallas kernels, body(): pl.pallas_call(functools.partial(kernel, n_x, n_z), out_shape=jax.ShapeDt...  85.3 us
    unnamed x15, local copies, waits for them, and re-layouts  3.7 us

profile of v3, /device:TPU:6, one launch (start us, length us, event | category | flops | bytes accessed | tf_op | source)
XLA Modules:
  0.0 93.3 jit_solution(11111882843437999001)
XLA Ops:
  0.0 0.9 %reshape.53 = bf16[2,200,64]{2,1,0:T(8,128)(2,1)S(1)} reshape(bf16[2,12800]{1,0:T(2,128)(2,1)} %param.8) | data formatting | bytes 102400 | tf_op jit(solution)/shard_map/reshape | solution.py:35
  1.0 0.1 reshape.52
  1.1 0.5 copy-done.4
  1.7 0.1 broadcast_multiply_fusion
  2.0 0.6 copy-done.3
  2.5 0.1 convolution_convert_fusion.1
  2.7 0.1 reshape.56
  2.9 0.1 reshape.57
  3.2 0.1 copy.25
  3.3 0.7 copy-done.2
  4.0 0.2 convert_reduce_fusion
  4.2 0.3 convolution_convert_fusion
  4.5 0.2 reshape.54
  4.6 0.1 copy.36
  4.8 0.1 reshape.55
  4.9 0.3 pad_maximum_fusion
  5.2 0.2 copy.30
  5.5 0.7 copy-done.5
  6.2 0.1 select_reduce_fusion
  6.4 0.1 reshape.59
  6.6 0.6 copy-done.6
  7.2 0.2 fusion.5.hot_id
  7.4 85.3 %shard_map.82 = f32[2,128]{1,0:T(2,128)S(1)} custom-call(bf16[16,4,16,128]{3,2,1,0:T(8,128)(2,1)S(1)} %pad.8.message, s32[16,4,1,128]{3,2,1,0:T(1,128)S(1)} %pad.9.ids, bf16[32,64,128]{2,1,0:T(8,128)(2,1)S(1)} %bitcast.20, s32[2]{0:T(128)S(1)} %fusion.5.hot_id), custom_call_target="tpu_custom_call" | custom-call | tf_op jit(solution)/shard_map/pallas_call | solution.py:437
  92.8 0.6 copy.40
  (23 shorter events, 0.6 us)
Async XLA Ops:
  0.0 1.0 %copy-start.1 = (bf16[2,12800]{1,0:T(2,128)(2,1)S(1)}, bf16[2,12800]{1,0:T(2,128)(2,1)}, u32[]{:S(2)}) copy-start(bf16[2,12800]{1,0:T(2,128)(2,1)} %param.9) | copy-start | bytes 153604
  1.0 0.7 copy-start.4
  1.9 0.7 copy-start.3
  3.3 0.7 copy-start.2
  5.4 2.0 %copy-start = (bf16[2048,128]{1,0:T(8,128)(2,1)S(1)}, bf16[2048,128]{1,0:T(8,128)(2,1)}, u32[]{:S(2)}) copy-start(bf16[2048,128]{1,0:T(8,128)(2,1)} %param.11) | copy-start | bytes 1572868
  5.5 0.7 copy-start.5
  6.6 0.7 copy-start.6

commit v4 on v3

--- a/solution.py
+++ b/solution.py
@@ -14,44 +14,26 @@
 PACKED_ROWS = 144
 ONE_ROWS = 80
 TWO_ROWS = PACKED_ROWS - ONE_ROWS
-LOTS_X = 4
+X_CUTS = (0, 1, 3, 5, 7, 11)
 LOTS_Z = 4
 MESH = pl.DeviceIdType.MESH
 bf16, f32, i32 = jnp.bfloat16, jnp.float32, jnp.int32
 
 
-def prepare(n_x, n_z, ratings, confidence, rated, cold_owner, cold_local, hot_group):
-    pairs = n_x * n_z
-    owners = cold_owner.reshape(-1)
-    local_ids = cold_local.reshape(-1)
-    cold = owners.shape[0]
-    order = jnp.arange(cold, dtype=i32)
-    same = (owners[:, None] == owners[None, :]) & (order[None, :] < order[:, None])
-    slot_of = jnp.sum(same.astype(i32), axis=1)
-    position = owners * CAP + slot_of
-    match = position[None, :] == jnp.arange(2 * pairs * CAP, dtype=i32)[:, None]
-    users = confidence.shape[0]
-    weights = confidence.reshape(users, -1, BLK) * rated.astype(bf16)[:, :, None]
-    both = jnp.concatenate([weights, ratings.reshape(users, -1, BLK)], axis=0)
-    both = both.transpose(1, 0, 2).reshape(-1, 2 * users * BLK)
-    cold_part = jnp.dot(match.astype(bf16), both[:cold], preferred_element_type=f32).astype(bf16)
-    cold_part = cold_part.reshape(n_x, n_z, 2 * CAP, 2 * users, BLK).transpose(1, 0, 3, 2, 4)
-    cold_part = cold_part.reshape(n_z, n_x, 2 * users, CAP, 2 * BLK)
-    hot_match = hot_group[None, :] == jnp.arange(2 * pairs, dtype=i32)[:, None]
-    hot_part = jnp.dot(hot_match.astype(bf16), both[cold:], preferred_element_type=f32).astype(bf16)
-    hot_part = hot_part.reshape(n_x, n_z, 2, 2 * users, BLK).transpose(1, 0, 3, 2, 4)
-    hot_part = hot_part.reshape(n_z, n_x, 2 * users, 1, 2 * BLK)
-    message = jnp.concatenate([cold_part, hot_part], axis=3).reshape(n_z, n_x, 6 * users, 2 * BLK)
-    message = jnp.pad(message, ((0, 0), (0, 0), (0, 16 - 6 * users), (0, 0)))
-    ids = jnp.sum(jnp.where(match, local_ids[None, :], 0), axis=1)
-    ids = ids.reshape(n_x, n_z, 1, 2 * CAP).transpose(1, 0, 2, 3)
-    ids = jnp.pad(ids, ((0, 0), (0, 0), (0, 0), (0, 128 - 2 * CAP)))
-    return message, ids
-
-
-def kernel(n_x, n_z, message, ids, items, hot_id, out,
-           table, msg_z, msg_x, ids_z, ids_x, ids_s, one, two, one_x_half, one_x, one_z_half, one_z,
-           two_z_half, two_z, two_x_half, two_x,
+def blocks_of(values):
+    users = values.shape[0]
+    values = values.reshape(users, -1, BLK)
+    return jnp.pad(values, ((0, 0), (0, -values.shape[1] % 128), (0, 0)))
+
+
+def row_of_all(cold, hot):
+    row = jnp.concatenate([cold.reshape(-1), hot])
+    return jnp.pad(row, (0, -row.shape[0] % 128))[None, :]
+
+
+def kernel(n_x, n_z, cold, listed, confidence, ratings, rated, owners, locals_, items, out,
+           table, staged, message, msg_z, passed, msg_x, ids, ids_z, ids_x, ids_s, one, two, one_x_half, one_x, one_z_half, one_z,
+           two_z_half, two_z, two_x,
            y_send, y_recv, c_send, c_recv, l_sem, a_send, a_recv, b_send, b_recv,
            one_x_sem, one_z_sem, two_z_sem, two_x_sem):
     dp = lax.axis_index("dp")
@@ -83,12 +65,50 @@
         return remote(ref, ref, send, recv, mate_id)
 
     barrier = pltpu.get_barrier_semaphore()
+    for k in sorted(range(1, n_z), key=lambda k: -min(k, n_z - k)):
+        pl.semaphore_signal(barrier, inc=1, device_id=at(x, (z + k) % n_z), device_id_type=MESH)
+    each(n_x, lambda k: pl.semaphore_signal(
+        barrier, inc=1, device_id=at((x + k) % n_x, z), device_id_type=MESH))
     for to in (up_id, down_id, mate_id):
         pl.semaphore_signal(barrier, inc=1, device_id=to, device_id_type=MESH)
-    each(n_z, lambda k: pl.semaphore_signal(
-        barrier, inc=1, device_id=at(x, (z + k) % n_z), device_id_type=MESH))
-    each(n_x, lambda k: pl.semaphore_signal(
-        barrier, inc=1, device_id=at((x + k) % n_x, z), device_id_type=MESH))
+
+    pairs = n_x * n_z
+    width = owners.shape[1]
+    owner_row = owners[...]
+    owner_col = jnp.broadcast_to(owner_row, (8, width)).T[:, :1]
+    before = lax.broadcasted_iota(i32, (width, width), 0) < lax.broadcasted_iota(i32, (width, width), 1)
+    slot = jnp.sum(jnp.where((owner_col == owner_row) & before, 1, 0), axis=0, keepdims=True)
+    number = lax.broadcasted_iota(i32, (1, width), 1)
+    key = jnp.where(number < cold, owner_row * CAP + slot, jnp.where(number < listed, owner_row + 2 * pairs, -1))
+
+    def wanted(pair, s):
+        return 4 * pair + s if s < 4 else 4 * pairs + 2 * pair + s - 4
+
+    entry = lax.broadcasted_iota(i32, (pairs, 1), 0)
+    pair_of = (entry % n_x) * n_z + entry // n_x
+    match = jnp.concatenate([key == wanted(pair_of, s) for s in range(6)], axis=0)
+    rating_pick = jnp.where(match, 1.0, 0.0).astype(bf16)
+    picked = []
+    for u in range(2):
+        weight_pick = jnp.where(match, rated[u:u + 1, :].astype(f32), 0.0).astype(bf16)
+        picked.append(jnp.dot(weight_pick, confidence[u], preferred_element_type=f32))
+    for u in range(2):
+        picked.append(jnp.dot(rating_pick, ratings[u], preferred_element_type=f32))
+    for n, lot in enumerate(picked):
+        for j in range(3):
+            both = [lot[(2 * j + i) * pairs:(2 * j + i + 1) * pairs] for i in range(2)]
+            staged[pl.ds(3 * n + j, pairs, stride=12), :] = jnp.concatenate(both, axis=1)
+    message[...] = staged[...].astype(bf16).reshape(message.shape)
+    to_z_entry = lax.broadcasted_iota(i32, (n_z, 1), 0)
+    lane = lax.broadcasted_iota(i32, (n_z, 128), 1)
+    id_rows = jnp.zeros((n_z, 128), i32)
+    for x_to in range(n_x):
+        for s in range(6):
+            hit = jnp.where(key == wanted(x_to * n_z + to_z_entry, s), locals_[...], 0)
+            id_rows = id_rows + jnp.where(lane == 8 * x_to + s, jnp.sum(hit, axis=1, keepdims=True), 0)
+    for z_to in range(n_z):
+        ids[z_to] = id_rows[z_to:z_to + 1]
+
     pl.semaphore_wait(barrier, 3 + n_z - 1 + n_x - 1)
 
     held = items.shape[0]
@@ -131,24 +151,55 @@
     keep = pltpu.make_async_copy(items, table.at[core, pl.ds(y * held, held)], l_sem.at[0])
     keep.start()
 
+    def place_of(k):
+        return 0 if 2 * k == n_z else (n_z - 2 * k if 2 * k < n_z else 2 * k - n_z - 1)
+
+    outer = n_z // 2 - 1
+    spans = (pl.ds(0, outer), pl.ds(outer, n_z - outer))
+    counts = (outer, n_z - outer - 1)
+
     def start_z(k):
         to = (z + k) % n_z
-        remote(message.at[to], msg_z.at[z], a_send.at[0], a_recv.at[0], at(x, to)).start()
-        remote(ids.at[to], ids_z.at[z], a_send.at[1], a_recv.at[1], at(x, to)).start()
-
-    def start_x(k):
+        lot = 0 if place_of(k) < outer else 1
+        remote(message.at[to], msg_z.at[place_of(k)], a_send.at[0, lot], a_recv.at[0, lot], at(x, to)).start()
+        remote(ids.at[to], ids_z.at[place_of(k)], a_send.at[1, lot], a_recv.at[1, lot], at(x, to)).start()
+
+    def start_x(k, lot):
         to = (x + k) % n_x
-        remote(msg_z.at[:, to], msg_x.at[x], b_send.at[0], b_recv.at[0], at(to, z)).start()
-        remote(ids_z.at[:, to], ids_x.at[x], b_send.at[1], b_recv.at[1], at(to, z)).start()
-
-    z_done = [waiter(others(msg_z), a_send.at[0], a_recv.at[0]), waiter(others(ids_z), a_send.at[1], a_recv.at[1])]
-    x_done = [waiter(others(msg_x), b_send.at[0], b_recv.at[0]), waiter(others(ids_x), b_send.at[1], b_recv.at[1])]
-
-    each(n_z, start_z)
+        remote(passed.at[to, spans[lot]], msg_x.at[x, spans[lot]], b_send.at[0, lot], b_recv.at[0, lot], at(to, z)).start()
+        remote(ids_z.at[spans[lot]], ids_x.at[x, spans[lot]], b_send.at[1, lot], b_recv.at[1, lot], at(to, z)).start()
+
+    z_done, x_done = [], []
+    for lot in range(2):
+        some = pl.ds(0, counts[lot])
+        z_done.append([waiter(msg_z.at[some], a_send.at[0, lot], a_recv.at[0, lot]),
+                       waiter(ids_z.at[some], a_send.at[1, lot], a_recv.at[1, lot])])
+        some = pl.ds(0, n_x - 1)
+        x_done.append([waiter(msg_x.at[some, spans[lot]], b_send.at[0, lot], b_recv.at[0, lot]),
+                       waiter(ids_x.at[some, spans[lot]], b_send.at[1, lot], b_recv.at[1, lot])])
+
+    def pass_on(lot):
+        for copy in z_done[lot]:
+            copy.wait_recv()
+
+        def part(n, carry):
+            text = msg_z[n].astype(f32)
+            for x_to in range(n_x):
+                rows_to = jnp.concatenate([text[12 * x_to:12 * x_to + 12], jnp.zeros((4, 128), f32)], axis=0)
+                passed[x_to, n] = rows_to.astype(bf16)
+            return carry
+
+        lax.fori_loop(spans[lot].start, spans[lot].start + spans[lot].size, part, 0)
+        each(n_x, lambda k: start_x(k, lot))
+        msg_x[x, spans[lot]] = passed[x, spans[lot]]
+        ids_x[x, spans[lot]] = ids_z[spans[lot]]
+
+    for k in sorted(range(1, n_z), key=place_of):
+        start_z(k)
     for h in range(2):
         mate_copy(h, own(h), y, h).start()
-    msg_z[z] = message[z]
-    ids_z[z] = ids[z]
+    msg_z[n_z - 1] = message[z]
+    ids_z[n_z - 1] = ids[z]
 
     from_down(0).wait_recv()
     up_copy(2).start()
@@ -157,18 +208,15 @@
     mate_copy(2, rows(core, down, 0), down, 0).start()
     mate_copy(3, rows(core, up, 1), up, 1).start()
 
-    for copy in z_done:
-        copy.wait_recv()
-    each(n_x, start_x)
-    msg_x[x] = msg_z[:, x]
-    ids_x[x] = ids_z[:, x]
+    pass_on(0)
+    pass_on(1)
 
     from_down(1).wait_recv()
     mate_copy(4, rows(core, down, 1), down, 1).start()
     from_up(1).wait_recv()
     mate_copy(5, rows(core, up, 0), up, 0).start()
 
-    for copy in x_done:
+    for copy in x_done[0] + x_done[1]:
         copy.wait_recv()
     to_smem = pltpu.make_async_copy(ids_x, ids_s, l_sem.at[1])
     to_smem.start()
@@ -178,7 +226,7 @@
     from_up(2).wait_recv()
     mate_copy(7, rows(core, far, 1), far, 1).start()
 
-    for copy in z_done + x_done:
+    for copy in z_done[0] + z_done[1] + x_done[0] + x_done[1]:
         copy.wait_send()
     for k in range(3):
         up_copy(k).wait_send()
@@ -191,27 +239,21 @@
     keep.wait()
     to_smem.wait()
 
-    hot_rows = [table[0, hot_id[0]], table[1, hot_id[1]]]
     row_of = lax.broadcasted_iota(i32, (16, 128), 0)
     masks = [((row_of == 6 + j) | (row_of == 9 + j)).astype(f32) for j in range(3)]
     lane_block = lax.broadcasted_iota(i32, (8, 128), 1) // 8
     window = [(lane_block >= i) & (lane_block < i + 8) for i in range(8)]
 
-    def z_at(place):
-        ahead = n_z // 2 - (place + 1) // 2
-        behind = n_z // 2 + place // 2
-        return (z + jnp.where(place % 2 == 1, ahead, behind)) % n_z
-
     def build(place, carry):
         for p in range(n_x):
             build_one(p, place)
         return carry
 
     def build_one(p, place):
-        xt, zt = (x + (2, 1, 3, 0)[p]) % n_x, z_at(place)
-        found = [table[s // CAP, ids_s[xt, zt, 0, s]] for s in range(2 * CAP)] + hot_rows
+        xt = (x + (2, 1, 3, 0)[p]) % n_x
+        found = [table[(0, 0, 1, 1, 0, 1)[s], ids_s[xt, place, 0, 8 * x + s]] for s in range(6)]
         chosen = jnp.concatenate(found, axis=0).T
-        text = msg_x[xt, zt].astype(f32)
+        text = msg_x[xt, place].astype(f32)
         scaled = []
         for u in range(2):
             weight = jnp.concatenate(
@@ -241,7 +283,9 @@
     last_x, last_z = n_x - 1, n_z - 1
     to_x = (at((x + 1) % n_x, z), at((x + n_x - 1) % n_x, z))
     to_z = (at(x, (z + 1) % n_z), at(x, (z + n_z - 1) % n_z))
-    quarter = n_z // LOTS_X
+    x_cuts = [cut for cut in X_CUTS if cut < n_z] + [n_z]
+    x_lots = [pl.ds(cut, after - cut) for cut, after in zip(x_cuts, x_cuts[1:])]
+    x_lot_of = [sum(cut <= n for cut in x_cuts) - 1 for n in range(n_z)]
     wide = n_x // LOTS_Z
     one_rows, two_rows = one.shape[2] // 2, two.shape[2] // 2
     steps_x, steps_z = n_x // 2, n_z // 2
@@ -252,7 +296,7 @@
         return 0 if step == 0 else 2 * step - 1 + way
 
     def one_x_copy(way, step, j):
-        lots = pl.ds(quarter * j, quarter)
+        lots = x_lots[j]
         sems = one_x_sem.at[0, way, step, j], one_x_sem.at[1, way, step, j]
         if step == 0:
             return remote(one.at[0, lots, pl.ds(one_rows * way, one_rows)], one_x_half.at[way, lots], *sems, to_x[way])
@@ -271,11 +315,10 @@
             return remote(two.at[lot, 0, pl.ds(two_rows * way, two_rows)], two_z_half.at[way, lot], *sems, to_z[way])
         return remote(two.at[lot, place(way, step, steps_z)], two_z.at[way, step - 1, lot], *sems, to_z[way])
 
-    def two_x_copy(way, step):
-        sems = two_x_sem.at[0, way, step], two_x_sem.at[1, way, step]
-        if step == 0:
-            return remote(two.at[0, last_z, pl.ds(two_rows * way, two_rows)], two_x_half.at[way], *sems, to_x[way])
-        return remote(two.at[place(way, step, steps_x), last_z], two_x.at[way, step - 1], *sems, to_x[way])
+    def two_x_copy(p):
+        ahead = (2, 1, 3)[p]
+        sems = two_x_sem.at[0, p], two_x_sem.at[1, p]
+        return remote(two.at[p, last_z], two_x.at[p], *sems, at((x + ahead) % n_x, z))
 
     delay, event_us, build_us = 2.5, 0.15, 0.5
     clock = {"now": 0.0, "x": 0.0, "z": 0.0}
@@ -289,7 +332,7 @@
     def start_one_x(step, j):
         for way in range(2):
             one_x_copy(way, step, j).start()
-        sent("x", quarter * one_rows * (2 if step else 1), one_x_event, (step, j))
+        sent("x", x_lots[j].size * one_rows * (2 if step else 1), one_x_event, (step, j))
 
     def start_one_z(step):
         for way in range(2):
@@ -301,15 +344,15 @@
             two_z_copy(way, step, p).start()
         sent("z", wide * two_rows * (2 if step else 1), two_z_event, (step, p))
 
-    def start_two_x(step):
-        for way in range(2):
-            two_x_copy(way, step).start()
-        sent("x", two_rows * (2 if step else 1), two_x_event, (step,))
+    def start_two_x():
+        for p in range(last_x):
+            two_x_copy(p).start()
+        sent("x", 4 * two_rows, two_x_event, ())
 
     def ready_one_z():
         step = len(done_z)
-        needed = max(place(way, step, steps_z) for way in range(2)) // quarter
-        if step < steps_z and needed in done_x and ("one", step) not in begun:
+        needed = x_lot_of[max(place(way, step, steps_z) for way in range(2))]
+        if step < steps_z and set(range(needed + 1)) <= set(done_x) and ("one", step) not in begun:
             begun.add(("one", step))
             start_one_z(step)
 
@@ -318,7 +361,7 @@
     def one_x_event(step, j):
         for way in range(2):
             one_x_copy(way, step, j).wait()
-            lots = pl.ds(quarter * j, quarter)
+            lots = x_lots[j]
             at_place = place(way, step + 1, steps_x)
             if step == 0:
                 one[at_place, lots, pl.ds(one_rows * way, one_rows)] += one_x_half[way, lots]
@@ -326,6 +369,8 @@
                 one[at_place, lots] += one_x[way, step - 1, lots]
         if step + 1 < steps_x:
             start_one_x(step + 1, j)
+            if j + 2 < len(x_lots):
+                first_one_x(j + 2)
         else:
             done_x.append(j)
             ready_one_z()
@@ -355,18 +400,12 @@
         if step + 1 < steps_z:
             start_two_z(step + 1, p)
         elif p == n_x // wide - 1:
-            start_two_x(0)
-
-    def two_x_event(step):
-        for way in range(2):
-            two_x_copy(way, step).wait()
-            at_place = place(way, step + 1, steps_x)
-            if step == 0:
-                two[at_place, last_z, pl.ds(two_rows * way, two_rows)] += two_x_half[way]
-            else:
-                two[at_place, last_z] += two_x[way, step - 1]
-        if step + 1 < steps_x:
-            start_two_x(step + 1)
+            start_two_x()
+
+    def two_x_event():
+        for p in range(last_x):
+            two_x_copy(p).wait()
+        two[last_x, last_z] += two_x[0] + two_x[1] + two_x[2]
 
     def build_some():
         first = built[0]
@@ -377,8 +416,14 @@
         if first == 0:
             for p in range(n_x // wide):
                 start_two_z(0, p)
-        if built[0] % quarter == 0:
-            start_one_x(0, built[0] // quarter - 1)
+        for j in range(min(2, len(x_lots))):
+            if first < x_cuts[j + 1] <= built[0]:
+                start_one_x(0, j)
+
+    def first_one_x(j):
+        while built[0] < x_cuts[j + 1]:
+            build_some()
+        start_one_x(0, j)
 
     while pending or built[0] < n_z:
         pending.sort()
@@ -426,24 +471,25 @@
 
 
 def body(n_x, n_z, ratings, confidence, rated, item_factors, cold_owner, cold_local, hot_group, hot_local):
-    message, ids = prepare(n_x, n_z, ratings, confidence, rated, cold_owner, cold_local, hot_group)
-    groups = lax.axis_index("dp") // 2 * 2 + jnp.arange(2, dtype=i32)
-    hot_id = jnp.sum(jnp.where(hot_group[None, :] == groups[:, None], hot_local[None, :], 0), axis=1)
     users = confidence.shape[0]
+    cold, listed = cold_owner.size, rated.shape[1]
     rows, width = item_factors.shape
     vmem = pl.BlockSpec(memory_space=pltpu.VMEM)
-    smem = pl.BlockSpec(memory_space=pltpu.SMEM)
     dma = pltpu.SemaphoreType.DMA
     return pl.pallas_call(
-        functools.partial(kernel, n_x, n_z),
+        functools.partial(kernel, n_x, n_z, cold, listed),
         out_shape=jax.ShapeDtypeStruct((users, width), f32),
-        in_specs=[vmem, vmem, pl.BlockSpec(memory_space=pl.ANY), smem],
+        in_specs=[vmem] * 5 + [pl.BlockSpec(memory_space=pl.ANY)],
         out_specs=vmem,
         scratch_shapes=[
             pltpu.VMEM((2, 4 * rows // BLK, BLK, width), bf16),
-            pltpu.VMEM((n_z, n_x, 16, width), bf16),
+            pltpu.VMEM((n_z * n_x * 12, width), f32),
+            pltpu.VMEM((n_z, n_x * 12, width), bf16),
+            pltpu.VMEM((n_z, n_x * 12, width), bf16),
             pltpu.VMEM((n_x, n_z, 16, width), bf16),
-            pltpu.VMEM((n_z, n_x, 1, 128), i32),
+            pltpu.VMEM((n_x, n_z, 16, width), bf16),
+            pltpu.VMEM((n_z, 1, 128), i32),
+            pltpu.VMEM((n_z, 1, 128), i32),
             pltpu.VMEM((n_x, n_z, 1, 128), i32),
             pltpu.SMEM((n_x, n_z, 1, 128), i32),
             pltpu.VMEM((n_x, n_z, ONE_ROWS, width), f32),
@@ -454,15 +500,18 @@
             pltpu.VMEM((2, n_z // 2 - 1, ONE_ROWS, width), f32),
             pltpu.VMEM((2, n_x, TWO_ROWS // 2, width), f32),
             pltpu.VMEM((2, n_z // 2 - 1, n_x, TWO_ROWS, width), f32),
-            pltpu.VMEM((2, TWO_ROWS // 2, width), f32),
-            pltpu.VMEM((2, n_x // 2 - 1, TWO_ROWS, width), f32),
+            pltpu.VMEM((n_x - 1, TWO_ROWS, width), f32),
             dma((6,)), dma((6,)), dma((8,)), dma((8,)), dma((2,)),
-            dma((2,)), dma((2,)), dma((2,)), dma((2,)),
-            dma((2, 2, n_x // 2, LOTS_X)), dma((2, 2, n_z // 2)), dma((2, 2, n_z // 2, LOTS_Z)), dma((2, 2, n_x // 2)),
+            dma((2, 2)), dma((2, 2)), dma((2, 2)), dma((2, 2)),
+            dma((2, 2, n_x // 2, len(X_CUTS))), dma((2, 2, n_z // 2)), dma((2, 2, n_z // 2, LOTS_Z)), dma((2, n_x - 1)),
         ],
         compiler_params=pltpu.CompilerParams(
             collective_id=0, has_side_effects=True, vmem_limit_bytes=40 * 1024 * 1024),
-    )(message, ids, item_factors.reshape(-1, BLK, width), hot_id)
+    )(
+        blocks_of(confidence), blocks_of(ratings),
+        jnp.pad(rated, ((0, 0), (0, -listed % 128))),
+        row_of_all(cold_owner, hot_group + 2 * n_x * n_z), row_of_all(cold_local, hot_local),
+        item_factors.reshape(-1, BLK, width))
 
 
 def solution(mesh):

time: 94.7 us -> 85.2 us (0.90); the launches traced: 93.3 us -> 84.9 us
  Pallas kernels: 85.3 us -> 79.5 us
  local copies, waits for them, and re-layouts: 6.32 us -> 5.23 us
    pallas_call x1, Pallas kernels: 85.3 us -> 79.5 us  [body(): pl.pallas_call(functools.partial(kernel, n_x, n_z, cold, listed), out_sha...]
    unnamed x15 -> x13, local copies, waits for them, and re-layouts: 3.7 us -> 3.22 us
    reshape x12 -> x2, local copies, waits for them, and re-layouts: 2.14 us -> 1.94 us  [blocks_of(): values = values.reshape(users, -1, BLK)]
where the time goes in v4:
time: 85.2 us; the launch traced here: 84.9 us
  Pallas kernels  79.5 us (93%)
  local copies, waits for them, and re-layouts  5.23 us (6%)
    pallas_call x1, Pallas kernels, body(): pl.pallas_call(functools.partial(kernel, n_x, n_z, cold, listed), out_sha...  79.5 us
    unnamed x13, local copies, waits for them, and re-layouts  3.22 us
    reshape x2, local copies, waits for them, and re-layouts, blocks_of(): values = values.reshape(users, -1, BLK)  1.94 us

profile of v4, /device:TPU:6, one launch (start us, length us, event | category | flops | bytes accessed | tf_op | source)
XLA Modules:
  0.0 84.9 jit_solution(17085593708044079365)
XLA Ops:
  0.0 0.0 copy-start
  0.0 1.0 %reshape.15 = bf16[2,200,64]{2,1,0:T(8,128)(2,1)S(1)} reshape(bf16[2,12800]{1,0:T(2,128)(2,1)} %param.9) | data formatting | bytes 102400 | tf_op jit(solution)/shard_map/reshape | solution.py:25
  1.0 0.9 %reshape.16 = bf16[2,200,64]{2,1,0:T(8,128)(2,1)S(1)} reshape(bf16[2,12800]{1,0:T(2,128)(2,1)} %param.8) | data formatting | bytes 102400 | tf_op jit(solution)/shard_map/reshape | solution.py:25
  2.0 0.0 copy-start.5
  2.0 0.6 copy-done.5
  2.7 0.0 copy-start.2
  2.7 0.7 copy-done.2
  3.3 0.1 pad_add_fusion
  3.4 0.0 copy-start.3
  3.4 0.0 copy-start.4
  3.4 0.7 copy-done.3
  4.1 0.0 copy-done.4
  4.1 0.1 pad_add_fusion.1
  4.2 0.0 copy-start.1
  4.2 0.7 copy-done.1
  4.9 0.0 copy-done
  4.9 79.5 %shard_map.82 = f32[2,128]{1,0:T(2,128)S(1)} custom-call(bf16[2,256,64]{2,1,0:T(8,128)(2,1)S(1)} %pad.18.confidence, bf16[2,256,64]{2,1,0:T(8,128)(2,1)S(1)} %pad.19.ratings, s32[2,256]{1,0:T(2,128)S(1)} %pad.20.rated, s32[1,256]{1,0:T(1,128)S(1)} %bitcast.6, s32[1,256]{1,0:T(1,128)S(1)} %bitcast.7, bf16[32,64,128]{2,1,0:T(8,128)(2,1)S(1)} %bitcast.5), custom_call_target="tpu_custom_call" | custom-call | tf_op jit(solution)/shard_map/pallas_call | solution.py:479
  84.4 0.6 copy.10
  (6 shorter events, 0.1 us)
Async XLA Ops:
  0.0 4.9 %copy-start = (bf16[2048,128]{1,0:T(8,128)(2,1)S(1)}, bf16[2048,128]{1,0:T(8,128)(2,1)}, u32[]{:S(2)}) copy-start(bf16[2048,128]{1,0:T(8,128)(2,1)} %param.11) | copy-start | bytes 1572868
  2.0 0.7 copy-start.5
  2.7 0.7 copy-start.2
  3.4 0.7 copy-start.3
  3.4 0.7 copy-start.4
  4.2 0.7 copy-start.1

commit v5 on v4

--- a/solution.py
+++ b/solution.py
@@ -20,18 +20,8 @@
 bf16, f32, i32 = jnp.bfloat16, jnp.float32, jnp.int32
 
 
-def blocks_of(values):
-    users = values.shape[0]
-    values = values.reshape(users, -1, BLK)
-    return jnp.pad(values, ((0, 0), (0, -values.shape[1] % 128), (0, 0)))
-
-
-def row_of_all(cold, hot):
-    row = jnp.concatenate([cold.reshape(-1), hot])
-    return jnp.pad(row, (0, -row.shape[0] % 128))[None, :]
-
-
-def kernel(n_x, n_z, cold, listed, confidence, ratings, rated, owners, locals_, items, out,
+def kernel(n_x, n_z, confidence_in, ratings_in, rated_in, owners_in, locals_in, hot_group_in, hot_local_in, items, out,
+           confidence, ratings, rated, owners, locals_, hot_group, hot_local, pairs_of, lined, in_sem,
            table, staged, message, msg_z, passed, msg_x, ids, ids_z, ids_x, ids_s, one, two, one_x_half, one_x, one_z_half, one_z,
            two_z_half, two_z, two_x,
            y_send, y_recv, c_send, c_recv, l_sem, a_send, a_recv, b_send, b_recv,
@@ -72,9 +62,39 @@
     for to in (up_id, down_id, mate_id):
         pl.semaphore_signal(barrier, inc=1, device_id=to, device_id_type=MESH)
 
+    given = (confidence_in, ratings_in, rated_in, owners_in, locals_in, hot_group_in, hot_local_in)
+    held_in = (confidence, ratings, rated, owners, locals_, hot_group, hot_local)
+    inputs = [pltpu.make_async_copy(a, b, in_sem.at[n]) for n, (a, b) in enumerate(zip(given, held_in))]
+    for copy in inputs:
+        copy.start()
+
     pairs = n_x * n_z
-    width = owners.shape[1]
-    owner_row = owners[...]
+    for copy in inputs:
+        copy.wait()
+    cold, hot = owners.shape[1], hot_group.shape[1]
+    listed = cold + hot
+    width = listed + -listed % 128
+
+    def row_of(cold_part, hot_part):
+        return jnp.concatenate([cold_part, hot_part, jnp.zeros((1, width - listed), i32)], axis=1)
+
+    owner_row = row_of(owners[...], hot_group[...] + 2 * pairs)
+    local_row = row_of(locals_[...], hot_local[...])
+
+    def two_blocks(k, carry):
+        lanes = pl.ds(pl.multiple_of(128 * k, 128), 128)
+        for n, given in enumerate((confidence, ratings)):
+            lot = given[:, lanes].astype(f32)
+            for u in range(2):
+                pairs_of[2 * n + u, pl.ds(k, 1), :] = lot[u:u + 1]
+        return carry
+
+    lax.fori_loop(0, listed // 2, two_blocks, 0, unroll=4)
+    for n in range(4):
+        lined[n, pl.ds(listed, width - listed), :] = jnp.zeros((width - listed, 128), f32)
+        lot = pairs_of[n]
+        lined[n, pl.ds(0, listed // 2, stride=2), :] = lot
+        lined[n, pl.ds(1, listed // 2, stride=2), :] = jnp.concatenate([lot[:, BLK:], lot[:, :BLK]], axis=1)
     owner_col = jnp.broadcast_to(owner_row, (8, width)).T[:, :1]
     before = lax.broadcasted_iota(i32, (width, width), 0) < lax.broadcasted_iota(i32, (width, width), 1)
     slot = jnp.sum(jnp.where((owner_col == owner_row) & before, 1, 0), axis=0, keepdims=True)
@@ -90,13 +110,14 @@
     rating_pick = jnp.where(match, 1.0, 0.0).astype(bf16)
     picked = []
     for u in range(2):
-        weight_pick = jnp.where(match, rated[u:u + 1, :].astype(f32), 0.0).astype(bf16)
-        picked.append(jnp.dot(weight_pick, confidence[u], preferred_element_type=f32))
+        rated_row = jnp.concatenate([rated[u:u + 1, :], jnp.zeros((1, width - listed), i32)], axis=1)
+        weight_pick = jnp.where(match, rated_row.astype(f32), 0.0).astype(bf16)
+        picked.append(jnp.dot(weight_pick, lined[u].astype(bf16), preferred_element_type=f32))
     for u in range(2):
-        picked.append(jnp.dot(rating_pick, ratings[u], preferred_element_type=f32))
+        picked.append(jnp.dot(rating_pick, lined[2 + u].astype(bf16), preferred_element_type=f32))
     for n, lot in enumerate(picked):
         for j in range(3):
-            both = [lot[(2 * j + i) * pairs:(2 * j + i + 1) * pairs] for i in range(2)]
+            both = [lot[(2 * j + i) * pairs:(2 * j + i + 1) * pairs, :BLK] for i in range(2)]
             staged[pl.ds(3 * n + j, pairs, stride=12), :] = jnp.concatenate(both, axis=1)
     message[...] = staged[...].astype(bf16).reshape(message.shape)
     to_z_entry = lax.broadcasted_iota(i32, (n_z, 1), 0)
@@ -104,7 +125,7 @@
     id_rows = jnp.zeros((n_z, 128), i32)
     for x_to in range(n_x):
         for s in range(6):
-            hit = jnp.where(key == wanted(x_to * n_z + to_z_entry, s), locals_[...], 0)
+            hit = jnp.where(key == wanted(x_to * n_z + to_z_entry, s), local_row, 0)
             id_rows = id_rows + jnp.where(lane == 8 * x_to + s, jnp.sum(hit, axis=1, keepdims=True), 0)
     for z_to in range(n_z):
         ids[z_to] = id_rows[z_to:z_to + 1]
@@ -117,32 +138,40 @@
     def rows(of_core, of_y, h):
         return table.at[of_core, pl.ds(of_y * held + h * half, half)]
 
+    fourth = half // 2
+
+    def fourths(of_core, of_y, q):
+        return table.at[of_core, pl.ds(of_y * held + q * fourth, fourth)]
+
     def own(h):
         return items.at[pl.ds(h * half, half)]
 
     def up_copy(k):
         if k < 2:
             return remote(own(k), rows(core, y, k), y_send.at[k], y_recv.at[k], up_id)
-        return remote(rows(core, down, 0), rows(core, down, 0), y_send.at[2], y_recv.at[2], up_id)
+        return remote(fourths(core, down, k - 2), fourths(core, down, k - 2), y_send.at[k], y_recv.at[k], up_id)
 
     def down_copy(k):
         if k < 2:
-            return remote(own(1 - k), rows(core, y, 1 - k), y_send.at[3 + k], y_recv.at[3 + k], down_id)
-        return remote(rows(core, up, 1), rows(core, up, 1), y_send.at[5], y_recv.at[5], down_id)
+            return remote(own(1 - k), rows(core, y, 1 - k), y_send.at[4 + k], y_recv.at[4 + k], down_id)
+        return remote(fourths(core, up, k), fourths(core, up, k), y_send.at[4 + k], y_recv.at[4 + k], down_id)
 
     def from_down(k):
-        ref = rows(core, down, k) if k < 2 else rows(core, far, 0)
+        ref = rows(core, down, k) if k < 2 else fourths(core, far, k - 2)
         return remote(ref, ref, y_send.at[k], y_recv.at[k], up_id)
 
     def from_up(k):
-        ref = rows(core, up, 1 - k) if k < 2 else rows(core, far, 1)
-        return remote(ref, ref, y_send.at[3 + k], y_recv.at[3 + k], down_id)
+        ref = rows(core, up, 1 - k) if k < 2 else fourths(core, far, k)
+        return remote(ref, ref, y_send.at[4 + k], y_recv.at[4 + k], down_id)
+
+    def lot_of(n, of_core, of_y, h):
+        return rows(of_core, of_y, h) if n < 6 else fourths(of_core, of_y, h)
 
     def mate_copy(n, src, of_y, h):
-        return remote(src, rows(core, of_y, h), c_send.at[n], c_recv.at[n], mate_id)
+        return remote(src, lot_of(n, core, of_y, h), c_send.at[n], c_recv.at[n], mate_id)
 
     def from_mate(n, of_y, h):
-        ref = rows(1 - core, of_y, h)
+        ref = lot_of(n, 1 - core, of_y, h)
         return remote(ref, ref, c_send.at[n], c_recv.at[n], mate_id)
 
     for k in range(2):
@@ -203,8 +232,10 @@
 
     from_down(0).wait_recv()
     up_copy(2).start()
+    up_copy(3).start()
     from_up(0).wait_recv()
     down_copy(2).start()
+    down_copy(3).start()
     mate_copy(2, rows(core, down, 0), down, 0).start()
     mate_copy(3, rows(core, up, 1), up, 1).start()
 
@@ -221,19 +252,20 @@
     to_smem = pltpu.make_async_copy(ids_x, ids_s, l_sem.at[1])
     to_smem.start()
 
-    from_down(2).wait_recv()
-    mate_copy(6, rows(core, far, 0), far, 0).start()
-    from_up(2).wait_recv()
-    mate_copy(7, rows(core, far, 1), far, 1).start()
+    for k in range(2):
+        from_down(2 + k).wait_recv()
+        mate_copy(6 + 2 * k, fourths(core, far, k), far, k).start()
+        from_up(2 + k).wait_recv()
+        mate_copy(7 + 2 * k, fourths(core, far, 2 + k), far, 2 + k).start()
 
     for copy in z_done[0] + z_done[1] + x_done[0] + x_done[1]:
         copy.wait_send()
-    for k in range(3):
+    for k in range(4):
         up_copy(k).wait_send()
         down_copy(k).wait_send()
-    halves = [(y, 0), (y, 1), (down, 0), (up, 1), (down, 1), (up, 0), (far, 0), (far, 1)]
+    halves = [(y, 0), (y, 1), (down, 0), (up, 1), (down, 1), (up, 0), (far, 0), (far, 2), (far, 1), (far, 3)]
     for n, (of_y, h) in enumerate(halves):
-        mate_copy(n, rows(core, of_y, h), of_y, h).wait_send()
+        mate_copy(n, lot_of(n, core, of_y, h), of_y, h).wait_send()
     for n, (of_y, h) in enumerate(halves):
         from_mate(n, of_y, h).wait_recv()
     keep.wait()
@@ -472,16 +504,22 @@
 
 def body(n_x, n_z, ratings, confidence, rated, item_factors, cold_owner, cold_local, hot_group, hot_local):
     users = confidence.shape[0]
-    cold, listed = cold_owner.size, rated.shape[1]
+    small = (confidence, ratings, rated, cold_owner.reshape(1, -1), cold_local.reshape(1, -1),
+             hot_group.reshape(1, -1), hot_local.reshape(1, -1))
+    listed = rated.shape[1]
+    lines = listed + -listed % 128
     rows, width = item_factors.shape
     vmem = pl.BlockSpec(memory_space=pltpu.VMEM)
     dma = pltpu.SemaphoreType.DMA
     return pl.pallas_call(
-        functools.partial(kernel, n_x, n_z, cold, listed),
+        functools.partial(kernel, n_x, n_z),
         out_shape=jax.ShapeDtypeStruct((users, width), f32),
-        in_specs=[vmem] * 5 + [pl.BlockSpec(memory_space=pl.ANY)],
+        in_specs=[pl.BlockSpec(memory_space=pl.ANY)] * 8,
         out_specs=vmem,
-        scratch_shapes=[
+        scratch_shapes=[pltpu.VMEM(a.shape, a.dtype) for a in small] + [
+            pltpu.VMEM((2 * users, listed // 2, width), f32),
+            pltpu.VMEM((2 * users, lines, width), f32),
+            dma((len(small),)),
             pltpu.VMEM((2, 4 * rows // BLK, BLK, width), bf16),
             pltpu.VMEM((n_z * n_x * 12, width), f32),
             pltpu.VMEM((n_z, n_x * 12, width), bf16),
@@ -501,17 +539,13 @@
             pltpu.VMEM((2, n_x, TWO_ROWS // 2, width), f32),
             pltpu.VMEM((2, n_z // 2 - 1, n_x, TWO_ROWS, width), f32),
             pltpu.VMEM((n_x - 1, TWO_ROWS, width), f32),
-            dma((6,)), dma((6,)), dma((8,)), dma((8,)), dma((2,)),
+            dma((8,)), dma((8,)), dma((10,)), dma((10,)), dma((2,)),
             dma((2, 2)), dma((2, 2)), dma((2, 2)), dma((2, 2)),
             dma((2, 2, n_x // 2, len(X_CUTS))), dma((2, 2, n_z // 2)), dma((2, 2, n_z // 2, LOTS_Z)), dma((2, n_x - 1)),
         ],
         compiler_params=pltpu.CompilerParams(
             collective_id=0, has_side_effects=True, vmem_limit_bytes=40 * 1024 * 1024),
-    )(
-        blocks_of(confidence), blocks_of(ratings),
-        jnp.pad(rated, ((0, 0), (0, -listed % 128))),
-        row_of_all(cold_owner, hot_group + 2 * n_x * n_z), row_of_all(cold_local, hot_local),
-        item_factors.reshape(-1, BLK, width))
+    )(*small, item_factors.reshape(-1, BLK, width))
 
 
 def solution(mesh):

time: 85.2 us -> 83.4 us (0.979)
  local copies, waits for them, and re-layouts: 5.23 us -> 3.92 us
    reshape x2 -> x0, local copies, waits for them, and re-layouts: 1.94 us -> none  [blocks_of(): values = values.reshape(users, -1, BLK)]
    unnamed x13 -> x17, local copies, waits for them, and re-layouts: 3.22 us -> 3.92 us
where the time goes in v5:
time: 83.4 us; the launch traced here: 83.1 us
  Pallas kernels  79.2 us (95%)
  local copies, waits for them, and re-layouts  3.92 us (5%)
    pallas_call x1, Pallas kernels, body(): pl.pallas_call(functools.partial(kernel, n_x, n_z), out_shape=jax.ShapeDt...  79.2 us
    unnamed x17, local copies, waits for them, and re-layouts  3.92 us

profile of v5, /device:TPU:6, one launch (start us, length us, event | category | flops | bytes accessed | tf_op | source)
XLA Modules:
  0.0 83.1 jit_solution(5429897838679316354)
XLA Ops:
  0.0 0.0 copy-start.5
  0.0 0.0 copy-start.7
  0.0 0.0 copy-start.3
  0.0 0.0 copy-start.4
  0.0 0.0 copy-start.6
  0.0 0.7 copy-done.5
  0.7 0.0 copy-done.7
  0.7 0.0 copy-done.3
  0.7 0.0 copy-done.4
  0.7 0.0 copy-done.6
  0.7 0.0 copy-start
  0.7 1.0 %copy-done = bf16[2048,128]{1,0:T(8,128)(2,1)S(1)} copy-done((bf16[2048,128]{1,0:T(8,128)(2,1)S(1)}, bf16[2048,128]{1,0:T(8,128)(2,1)}, u32[]{:S(2)}) %copy-start) | copy-done | bytes 524312
  1.8 0.0 copy-start.1
  1.8 0.8 copy-done.1
  2.6 0.0 copy-start.2
  2.6 0.8 copy-done.2
  3.4 79.2 %shard_map.82 = f32[2,128]{1,0:T(2,128)S(1)} custom-call(bf16[2,12800]{1,0:T(2,128)(2,1)S(1)} %copy-done.1, bf16[2,12800]{1,0:T(2,128)(2,1)S(1)} %copy-done.2, s32[2,200]{1,0:T(2,128)S(1)} %copy-done.3, s32[1,192]{1,0:T(1,128)S(1)} %bitcast.6, s32[1,192]{1,0:T(1,128)S(1)} %bitcast.7, s32[1,8]{1,0:T(1,128)S(1)} %bitcast.8, s32[1,8]{1,0:T(1,128)S(1)} %bitcast.9, ...), custom_call_target="tpu_custom_call" | custom-call | tf_op jit(solution)/shard_map/pallas_call | solution.py:514
  82.6 0.6 copy.10
Async XLA Ops:
  0.0 0.7 copy-start.5
  0.0 0.7 copy-start.7
  0.0 0.7 copy-start.3
  0.0 0.7 copy-start.4
  0.0 0.7 copy-start.6
  0.7 1.0 %copy-start = (bf16[2048,128]{1,0:T(8,128)(2,1)S(1)}, bf16[2048,128]{1,0:T(8,128)(2,1)}, u32[]{:S(2)}) copy-start(bf16[2048,128]{1,0:T(8,128)(2,1)} %param.11) | copy-start | bytes 1572868
  1.8 0.8 copy-start.1
  2.6 0.8 copy-start.2

commit v6 on v5

--- a/solution.py
+++ b/solution.py
@@ -392,15 +392,19 @@
 
     def one_x_event(step, j):
         for way in range(2):
-            one_x_copy(way, step, j).wait()
+            one_x_copy(way, step, j).wait_recv()
             lots = x_lots[j]
             at_place = place(way, step + 1, steps_x)
             if step == 0:
                 one[at_place, lots, pl.ds(one_rows * way, one_rows)] += one_x_half[way, lots]
             else:
                 one[at_place, lots] += one_x[way, step - 1, lots]
+            if step + 1 < steps_x:
+                one_x_copy(way, step + 1, j).start()
+        for way in range(2):
+            one_x_copy(way, step, j).wait_send()
         if step + 1 < steps_x:
-            start_one_x(step + 1, j)
+            sent("x", x_lots[j].size * one_rows * 2, one_x_event, (step + 1, j))
             if j + 2 < len(x_lots):
                 first_one_x(j + 2)
         else:
@@ -421,7 +425,7 @@
     def two_z_event(step, p):
         lot = pl.ds(p * wide, wide)
         for way in range(2):
-            two_z_copy(way, step, p).wait()
+            two_z_copy(way, step, p).wait_recv()
             at_place = place(way, step + 1, steps_z)
             while at_place >= built[0]:
                 build_some()
@@ -429,8 +433,12 @@
                 two[lot, at_place, pl.ds(two_rows * way, two_rows)] += two_z_half[way, lot]
             else:
                 two[lot, at_place] += two_z[way, step - 1, lot]
+            if step + 1 < steps_z:
+                two_z_copy(way, step + 1, p).start()
+        for way in range(2):
+            two_z_copy(way, step, p).wait_send()
         if step + 1 < steps_z:
-            start_two_z(step + 1, p)
+            sent("z", wide * two_rows * 2, two_z_event, (step + 1, p))
         elif p == n_x // wide - 1:
             start_two_x()
 

time: 83.4 us -> 83.6 us (level)
  no operation moved by 1% of the time
where the time goes in v6:
time: 83.6 us; the launch traced here: 83.3 us
  Pallas kernels  79.3 us (95%)
  local copies, waits for them, and re-layouts  3.92 us (5%)
    pallas_call x1, Pallas kernels, body(): pl.pallas_call(functools.partial(kernel, n_x, n_z), out_shape=jax.ShapeDt...  79.3 us
    unnamed x17, local copies, waits for them, and re-layouts  3.92 us

profile of v6, /device:TPU:6, one launch (start us, length us, event | category | flops | bytes accessed | tf_op | source)
XLA Modules:
  0.0 83.3 jit_solution(17386812220588379937)
XLA Ops:
  0.0 0.0 copy-start.5
  0.0 0.0 copy-start.7
  0.0 0.0 copy-start.3
  0.0 0.0 copy-start.4
  0.0 0.0 copy-start.6
  0.0 0.7 copy-done.5
  0.7 0.0 copy-done.7
  0.7 0.0 copy-done.3
  0.7 0.0 copy-done.4
  0.7 0.0 copy-done.6
  0.7 0.0 copy-start
  0.7 1.0 %copy-done = bf16[2048,128]{1,0:T(8,128)(2,1)S(1)} copy-done((bf16[2048,128]{1,0:T(8,128)(2,1)S(1)}, bf16[2048,128]{1,0:T(8,128)(2,1)}, u32[]{:S(2)}) %copy-start) | copy-done | bytes 524312
  1.8 0.0 copy-start.1
  1.8 0.8 copy-done.1
  2.6 0.0 copy-start.2
  2.6 0.8 copy-done.2
  3.4 79.3 %shard_map.82 = f32[2,128]{1,0:T(2,128)S(1)} custom-call(bf16[2,12800]{1,0:T(2,128)(2,1)S(1)} %copy-done.1, bf16[2,12800]{1,0:T(2,128)(2,1)S(1)} %copy-done.2, s32[2,200]{1,0:T(2,128)S(1)} %copy-done.3, s32[1,192]{1,0:T(1,128)S(1)} %bitcast.6, s32[1,192]{1,0:T(1,128)S(1)} %bitcast.7, s32[1,8]{1,0:T(1,128)S(1)} %bitcast.8, s32[1,8]{1,0:T(1,128)S(1)} %bitcast.9, ...), custom_call_target="tpu_custom_call" | custom-call | tf_op jit(solution)/shard_map/pallas_call | solution.py:522
  82.7 0.6 copy.10
Async XLA Ops:
  0.0 0.7 copy-start.5
  0.0 0.7 copy-start.7
  0.0 0.7 copy-start.3
  0.0 0.7 copy-start.4
  0.0 0.7 copy-start.6
  0.7 1.0 %copy-start = (bf16[2048,128]{1,0:T(8,128)(2,1)S(1)}, bf16[2048,128]{1,0:T(8,128)(2,1)}, u32[]{:S(2)}) copy-start(bf16[2048,128]{1,0:T(8,128)(2,1)} %param.11) | copy-start | bytes 1572868
  1.8 0.8 copy-start.1
  2.6 0.8 copy-start.2
